TPU v7x, 32 devices: a whole 2x2x4 slice. The times are simulated.
32 devices in a mesh: ctx: 8 (over z, x), grp: 4 (over y, core).
Axes of the slice: x: 2, y: 2, z: 4, core: 2. Of those that a mesh axis runs over, the one named last changes fastest.
Arguments:
- queries: bfloat16 [4096, 1024], P(('grp', 'ctx')), parts along dimension 0, may hold values from -160 to 160
- key_states: bfloat16 [4096, 128], P(('grp', 'ctx')), parts along dimension 0, may hold values from -7 to 7
- value_states: bfloat16 [4096, 128], P(('grp', 'ctx')), parts along dimension 0, may hold values from -6 to 6
- out_grad: bfloat16 [4096, 1024], P(('grp', 'ctx')), parts along dimension 0, may hold values from -6 to 6
- doc_ids: int32 [4096], P('grp'), parts along dimension 0, may hold values from 0 to 15, never falling along the last dimension, each value on 1 to 128 neighbouring positions
Outputs:
- attn_out: bfloat16 [4096, 1024], P(('grp', 'ctx')), parts along dimension 0
- query_grad: bfloat16 [4096, 1024], P(('grp', 'ctx')), parts along dimension 0
- key_grad: float32 [4096, 128], P(('grp', 'ctx')), parts along dimension 0
- value_grad: float32 [4096, 128], P(('grp', 'ctx')), parts along dimension 0
There are 4 independent parts, one for each index of `grp`. A program takes and returns all parts, laid end to end along the dimension named above; each array names one. Nothing has to cross between parts.
Inputs may be any that keep to these rules, and one draw needn't show every extreme that they name: `doc_ids`: nondecreasing along the sequence; each document covers 1 to 128 consecutive tokens, one exactly 128.
All inputs are finite; a program needn't handle non-finite values.
Results may differ from a plain program's by a relative error of at most 0.03.
Values may be sent and summed in bfloat16 or wider, within the bound.
A program may use at most 64 MiB of HBM per device.

v0:
```python
import math

import jax
import jax.numpy as jnp
from jax import lax
from jax.sharding import PartitionSpec as P

NEG_FILL = -1e30


def shifted(block, axis, distance):
    devices = range(lax.axis_size(axis))
    route = [(i - distance, i) for i in devices if i - distance in devices]
    return lax.ppermute(block, axis, route)


def piece_order(members, device, local_rows):
    upper_half = device * (local_rows // members) // (local_rows // 2)
    target = lax.broadcasted_iota(jnp.int32, (members,), 0)
    source_stretch = jnp.where(target % 2 == upper_half, target, 2 * members - 1 - target)
    return (source_stretch - upper_half) // 2


def relayout(arrays, spread_call, collect_call):
    members = lax.axis_size("ctx")
    device = lax.axis_index("ctx")
    local_rows = arrays[0].shape[0]
    pieces = tuple(
        (
            array_now.reshape(members, local_rows // members, array_now.shape[1])
            for array_now in arrays
        )
    )
    spread = spread_call(pieces)
    sources = piece_order(members, device, local_rows)
    regrouped = tuple((jnp.take(array_now, sources, axis=0) for array_now in spread))
    collected = collect_call(regrouped)
    settled = []
    for array_now in collected:
        joined = array_now.reshape(local_rows, array_now.shape[2])
        settled.append(
            jnp.where(device % 2 == 1, jnp.roll(joined, local_rows // 2, axis=0), joined)
        )
    return tuple(settled)


def fetch_lower(block_pair, hop_count):

    def advance(current, unused):
        arrived_now = shifted(current, "ctx", 1)
        return (arrived_now, arrived_now)

    remains, arrived = lax.scan(advance, block_pair, None, length=hop_count)
    return arrived


def fetch_higher(block_pair, hop_count):

    def advance(current, unused):
        arrived_now = shifted(current, "ctx", -1)
        return (arrived_now, arrived_now)

    remains, arrived = lax.scan(advance, block_pair, None, length=hop_count)
    return arrived


def return_lower(grad_pieces):

    def advance(running, piece_now):
        arrived_now = shifted(running + piece_now, "ctx", -1)
        return (arrived_now, None)

    returned, unused = lax.scan(advance, jnp.zeros_like(grad_pieces[0]), grad_pieces)
    return returned


def return_higher(grad_pieces):

    def advance(running, piece_now):
        arrived_now = shifted(running + piece_now, "ctx", 1)
        return (arrived_now, None)

    returned, unused = lax.scan(advance, jnp.zeros_like(grad_pieces[0]), grad_pieces)
    return returned


def attend(query_local, grad_local, window, own_stretches, locate, doc_all, reach_stretches):
    stretch_rows = query_local.shape[0] // 2
    head_dim = window.shape[-1]
    head_count = query_local.shape[1] // head_dim
    scaling = 1.0 / math.sqrt(head_dim)
    positions = lax.broadcasted_iota(jnp.int32, (stretch_rows,), 0)
    grad_window = jnp.zeros(window.shape, jnp.float32)
    out_parts = []
    query_parts = []
    for local_slot in range(2):
        query_stretch = own_stretches[local_slot]
        query_blk = query_local[
            local_slot * stretch_rows : (local_slot + 1) * stretch_rows
        ].reshape(stretch_rows, head_count, head_dim)
        grad_blk = grad_local[local_slot * stretch_rows : (local_slot + 1) * stretch_rows].reshape(
            stretch_rows, head_count, head_dim
        )
        query_doc = lax.dynamic_slice_in_dim(doc_all, query_stretch * stretch_rows, stretch_rows, 0)
        query_pos = query_stretch * stretch_rows + positions

        def tile_needed(distance, query_stretch=query_stretch, query_doc=query_doc):
            key_stretch = query_stretch - distance
            safe_stretch = jnp.maximum(key_stretch, 0)
            last_doc = lax.dynamic_slice_in_dim(
                doc_all, safe_stretch * stretch_rows + stretch_rows - 1, 1, 0
            )[0]
            return (key_stretch >= 0) & ((distance == 0) | (last_doc == query_doc[0]))

        def tile_scores(
            distance,
            query_stretch=query_stretch,
            query_doc=query_doc,
            query_pos=query_pos,
            query_blk=query_blk,
        ):
            key_stretch = query_stretch - distance
            window_pos, key_slot = locate(key_stretch)
            safe_stretch = jnp.maximum(key_stretch, 0)
            key_doc = lax.dynamic_slice_in_dim(
                doc_all, safe_stretch * stretch_rows, stretch_rows, 0
            )
            key_pos = key_stretch * stretch_rows + positions
            allowed = (key_doc[None, :] == query_doc[:, None]) & (
                key_pos[None, :] <= query_pos[:, None]
            )
            corner = (window_pos, key_slot, 0, 0, 0)
            kv_block = lax.dynamic_slice(window, corner, (1, 1, 2, stretch_rows, head_dim))[0, 0]
            scores = scaling * jnp.einsum(
                "thd,ud->htu", query_blk, kv_block[0], preferred_element_type=jnp.float32
            )
            scores = jnp.where(allowed[None], scores, NEG_FILL)
            return (scores, kv_block, corner)

        def max_step(distance, state):

            def max_compute_tile(current):
                row_max, row_sum = current
                scores, kv_block, corner = tile_scores(distance)
                new_max = jnp.maximum(row_max, jnp.max(scores, axis=2))
                new_sum = row_sum * jnp.exp(row_max - new_max) + jnp.sum(
                    jnp.exp(scores - new_max[:, :, None]), axis=2
                )
                return (new_max, new_sum)

            return lax.cond(tile_needed(distance), max_compute_tile, lambda current: current, state)

        initial = (
            jnp.full((head_count, stretch_rows), NEG_FILL, jnp.float32),
            jnp.zeros((head_count, stretch_rows), jnp.float32),
        )
        row_max, row_sum = lax.fori_loop(0, reach_stretches + 1, max_step, initial)
        log_total = row_max + jnp.log(row_sum)

        def out_step(distance, out_acc, log_total=log_total):

            def out_compute_tile(current):
                scores, kv_block, corner = tile_scores(distance)
                prob_bf = jnp.exp(scores - log_total[:, :, None]).astype(jnp.bfloat16)
                return current + jnp.einsum(
                    "htu,ud->htd", prob_bf, kv_block[1], preferred_element_type=jnp.float32
                )

            return lax.cond(
                tile_needed(distance), out_compute_tile, lambda current: current, out_acc
            )

        out_zero = jnp.zeros((head_count, stretch_rows, head_dim), jnp.float32)
        attn_heads = lax.fori_loop(0, reach_stretches + 1, out_step, out_zero).astype(jnp.bfloat16)
        grad_heads = grad_blk.transpose(1, 0, 2).astype(jnp.float32)
        row_dot = jnp.sum(grad_heads * attn_heads.astype(jnp.float32), axis=2)

        def back_step(
            distance,
            state,
            log_total=log_total,
            row_dot=row_dot,
            grad_blk=grad_blk,
            query_blk=query_blk,
        ):

            def back_compute_tile(current):
                query_acc, grad_acc = current
                scores, kv_block, corner = tile_scores(distance)
                weights = jnp.exp(scores - log_total[:, :, None])
                prob_bf = weights.astype(jnp.bfloat16)
                dprobs = jnp.einsum(
                    "thd,ud->htu", grad_blk, kv_block[1], preferred_element_type=jnp.float32
                )
                dscores = (weights * (dprobs - row_dot[:, :, None])).astype(jnp.bfloat16)
                query_acc = query_acc + scaling * jnp.einsum(
                    "htu,ud->htd", dscores, kv_block[0], preferred_element_type=jnp.float32
                )
                key_term = scaling * jnp.einsum(
                    "htu,thd->ud", dscores, query_blk, preferred_element_type=jnp.float32
                )
                value_term = jnp.einsum(
                    "htu,thd->ud", prob_bf, grad_blk, preferred_element_type=jnp.float32
                )
                present = lax.dynamic_slice(grad_acc, corner, (1, 1, 2, stretch_rows, head_dim))
                grad_acc = lax.dynamic_update_slice(
                    grad_acc, present + jnp.stack([key_term, value_term])[None, None], corner
                )
                return (query_acc, grad_acc)

            return lax.cond(
                tile_needed(distance), back_compute_tile, lambda current: current, state
            )

        query_acc, grad_window = lax.fori_loop(
            0, reach_stretches + 1, back_step, (out_zero, grad_window)
        )
        out_parts.append(attn_heads.transpose(1, 0, 2).reshape(stretch_rows, head_count * head_dim))
        query_parts.append(
            query_acc.astype(jnp.bfloat16)
            .transpose(1, 0, 2)
            .reshape(stretch_rows, head_count * head_dim)
        )
    return (jnp.concatenate(out_parts, axis=0), jnp.concatenate(query_parts, axis=0), grad_window)


def shards(queries, key_states, value_states, out_grad, doc_ids):
    members = lax.axis_size("ctx")
    device = lax.axis_index("ctx")
    reach_stretches = members // 4
    local_rows = queries.shape[0]
    stretch_rows = local_rows // 2
    head_dim = key_states.shape[1]
    query_local, grad_local, key_local, value_local = relayout(
        (queries, out_grad, key_states, value_states),
        lambda arranged: (
            lax.all_to_all(arranged[0], "ctx", split_axis=0, concat_axis=0, tiled=True),
            lax.all_to_all(arranged[1], "ctx", split_axis=0, concat_axis=0, tiled=True),
            lax.all_to_all(arranged[2], "ctx", split_axis=0, concat_axis=0, tiled=True),
            lax.all_to_all(arranged[3], "ctx", split_axis=0, concat_axis=0, tiled=True),
        ),
        lambda arranged: (
            lax.all_to_all(arranged[0], "ctx", split_axis=0, concat_axis=0, tiled=True),
            lax.all_to_all(arranged[1], "ctx", split_axis=0, concat_axis=0, tiled=True),
            lax.all_to_all(arranged[2], "ctx", split_axis=0, concat_axis=0, tiled=True),
            lax.all_to_all(arranged[3], "ctx", split_axis=0, concat_axis=0, tiled=True),
        ),
    )
    pair_local = jnp.stack(
        [
            key_local.reshape(2, stretch_rows, head_dim),
            value_local.reshape(2, stretch_rows, head_dim),
        ],
        axis=1,
    )
    lower_pairs = fetch_lower(pair_local, reach_stretches)
    higher_pairs = fetch_higher(pair_local, reach_stretches)
    window = jnp.concatenate([lower_pairs[::-1], pair_local[None], higher_pairs], axis=0)

    def locate(key_stretch):
        owner = jnp.where(key_stretch < members, key_stretch, 2 * members - 1 - key_stretch)
        return (owner - device + reach_stretches, (key_stretch >= members).astype(jnp.int32))

    own_stretches = (device, 2 * members - 1 - device)
    attn_out, query_grad, grad_window = attend(
        query_local, grad_local, window, own_stretches, locate, doc_ids, reach_stretches
    )
    returned = (
        grad_window[reach_stretches]
        + return_lower(grad_window[:reach_stretches])
        + return_higher(grad_window[reach_stretches + 1 :][::-1])
    )
    key_grad = returned[:, 0].reshape(local_rows, head_dim)
    value_grad = returned[:, 1].reshape(local_rows, head_dim)
    return (attn_out, query_grad, key_grad, value_grad)


def solution(mesh):
    placed = (
        P(("grp", "ctx"), None),
        P(("grp", "ctx"), None),
        P(("grp", "ctx"), None),
        P(("grp", "ctx"), None),
        P("grp"),
    )
    return jax.shard_map(
        shards,
        mesh=mesh,
        in_specs=placed,
        out_specs=(
            P(("grp", "ctx"), None),
            P(("grp", "ctx"), None),
            P(("grp", "ctx"), None),
            P(("grp", "ctx"), None),
        ),
        check_vma=False,
    )
```

profile of v0, /device:TPU:0, one launch (start us, length us, event | category | flops | bytes accessed | tf_op | source)
XLA Modules:
  0.0 176.7 jit_solution(10552287375855392524)
XLA Ops:
  0.6 7.3 %all-to-all-start = ((bf16[8,16,128]{2,1,0:T(8,128)(2,1)}), bf16[8,16,128]{2,1,0:T(8,128)(2,1)S(1)}, u32[]{:S(2)}, u32[]{:S(2)}) async-start(bf16[8,16,128]{2,1,0:T(8,128)(2,1)} %bitcast.338), calls=%async_computation | async-start | bytes 65536 | tf_op jit(solution)/shard_map/all_to_all | solution.py:239
  7.9 6.7 %all-to-all-done = bf16[8,16,128]{2,1,0:T(8,128)(2,1)S(1)} async-done(((bf16[8,16,128]{2,1,0:T(8,128)(2,1)}), bf16[8,16,128]{2,1,0:T(8,128)(2,1)S(1)}, u32[]{:S(2)}, u32[]{:S(2)}) %all-to-all-start) | async-done | bytes 32800 | tf_op jit(solution)/shard_map/all_to_all | solution.py:239
  14.6 3.3 %all-to-all-start.2 = ((bf16[8,16,128]{2,1,0:T(8,128)(2,1)}), bf16[8,16,128]{2,1,0:T(8,128)(2,1)S(1)}, u32[]{:S(2)}, u32[]{:S(2)}) async-start(bf16[8,16,128]{2,1,0:T(8,128)(2,1)} %bitcast.47), calls=%async_computation.2 | async-start | bytes 65536 | tf_op jit(solution)/shard_map/all_to_all | solution.py:240
  18.5 6.0 %all-to-all-done.2 = bf16[8,16,128]{2,1,0:T(8,128)(2,1)S(1)} async-done(((bf16[8,16,128]{2,1,0:T(8,128)(2,1)}), bf16[8,16,128]{2,1,0:T(8,128)(2,1)S(1)}, u32[]{:S(2)}, u32[]{:S(2)}) %all-to-all-start.2) | async-done | bytes 32800 | tf_op jit(solution)/shard_map/all_to_all | solution.py:240
  25.8 3.3 %all-to-all-start.3 = ((bf16[8,16,128]{2,1,0:T(8,128)(2,1)}), bf16[8,16,128]{2,1,0:T(8,128)(2,1)S(1)}, u32[]{:S(2)}, u32[]{:S(2)}) async-start(bf16[8,16,128]{2,1,0:T(8,128)(2,1)} %get-tuple-element.3063), calls=%async_computation.3 | async-start | bytes 65536 | tf_op jit(solution)/shard_map/all_to_all | solution.py:246
  29.2 6.6 %all-to-all-done.3 = bf16[8,16,128]{2,1,0:T(8,128)(2,1)S(1)} async-done(((bf16[8,16,128]{2,1,0:T(8,128)(2,1)}), bf16[8,16,128]{2,1,0:T(8,128)(2,1)S(1)}, u32[]{:S(2)}, u32[]{:S(2)}) %all-to-all-start.3) | async-done | bytes 32800 | tf_op jit(solution)/shard_map/all_to_all | solution.py:246
  35.8 3.5 %all-to-all-start.1 = ((bf16[8,16,128]{2,1,0:T(8,128)(2,1)}), bf16[8,16,128]{2,1,0:T(8,128)(2,1)S(1)}, u32[]{:S(2)}, u32[]{:S(2)}) async-start(bf16[8,16,128]{2,1,0:T(8,128)(2,1)} %get-tuple-element.3062), calls=%async_computation.1 | async-start | bytes 65536 | tf_op jit(solution)/shard_map/all_to_all | solution.py:245
  39.4 6.5 %all-to-all-done.1 = bf16[8,16,128]{2,1,0:T(8,128)(2,1)S(1)} async-done(((bf16[8,16,128]{2,1,0:T(8,128)(2,1)}), bf16[8,16,128]{2,1,0:T(8,128)(2,1)S(1)}, u32[]{:S(2)}, u32[]{:S(2)}) %all-to-all-start.1) | async-done | bytes 32800 | tf_op jit(solution)/shard_map/all_to_all | solution.py:245
  45.9 3.4 %all-to-all-start.6 = ((bf16[8,16,1024]{2,1,0:T(8,128)(2,1)}), bf16[8,16,1024]{2,1,0:T(8,128)(2,1)S(1)}, u32[]{:S(2)}, u32[]{:S(2)}) async-start(bf16[8,16,1024]{2,1,0:T(8,128)(2,1)} %bitcast.59), calls=%async_computation.6 | async-start | bytes 524288 | tf_op jit(solution)/shard_map/all_to_all | solution.py:238
  49.4 8.1 %all-to-all-done.6 = bf16[8,16,1024]{2,1,0:T(8,128)(2,1)S(1)} async-done(((bf16[8,16,1024]{2,1,0:T(8,128)(2,1)}), bf16[8,16,1024]{2,1,0:T(8,128)(2,1)S(1)}, u32[]{:S(2)}, u32[]{:S(2)}) %all-to-all-start.6) | async-done | bytes 262176 | tf_op jit(solution)/shard_map/all_to_all | solution.py:238
  57.5 3.4 %all-to-all-start.4 = ((bf16[8,16,1024]{2,1,0:T(8,128)(2,1)}), bf16[8,16,1024]{2,1,0:T(8,128)(2,1)S(1)}, u32[]{:S(2)}, u32[]{:S(2)}) async-start(bf16[8,16,1024]{2,1,0:T(8,128)(2,1)} %bitcast.53), calls=%async_computation.4 | async-start | bytes 524288 | tf_op jit(solution)/shard_map/all_to_all | solution.py:237
  61.5 7.5 %all-to-all-done.4 = bf16[8,16,1024]{2,1,0:T(8,128)(2,1)S(1)} async-done(((bf16[8,16,1024]{2,1,0:T(8,128)(2,1)}), bf16[8,16,1024]{2,1,0:T(8,128)(2,1)S(1)}, u32[]{:S(2)}, u32[]{:S(2)}) %all-to-all-start.4) | async-done | bytes 262176 | tf_op jit(solution)/shard_map/all_to_all | solution.py:237
  70.5 3.4 %all-to-all-start.5 = ((bf16[8,16,1024]{2,1,0:T(8,128)(2,1)}), bf16[8,16,1024]{2,1,0:T(8,128)(2,1)S(1)}, u32[]{:S(2)}, u32[]{:S(2)}) async-start(bf16[8,16,1024]{2,1,0:T(8,128)(2,1)} %get-tuple-element.3060), calls=%async_computation.5 | async-start | bytes 524288 | tf_op jit(solution)/shard_map/all_to_all | solution.py:243
  74.0 12.3 %while.166 = (s32[]{:T(128)}, bf16[2,2,64,128]{3,2,1,0:T(8,128)(2,1)S(1)}, bf16[2,2,2,64,128]{4,3,2,1,0:T(8,128)(2,1)S(1)}, s32[]{:T(128)}) while((s32[]{:T(128)}, bf16[2,2,64,128]{3,2,1,0:T(8,128)(2,1)S(1)}, bf16[2,2,2,64,128]{4,3,2,1,0:T(8,128)(2,1)S(1)}, s32[]{:T(128)}) %tuple.452), condition=%wide.region_1.3_spmd, body=%wide.region_0.2_spmd.sunk | while | flops 2 | bytes 524393 | solution.py:53
  74.0 3.8 %collective-permute-start = (bf16[2,2,64,128]{3,2,1,0:T(8,128)(2,1)S(1)}, bf16[2,2,64,128]{3,2,1,0:T(8,128)(2,1)S(1)}, u32[]{:S(2)}, u32[]{:S(2)}) collective-permute-start(bf16[2,2,64,128]{3,2,1,0:T(8,128)(2,1)S(1)} %get-tuple-element.3575), channel_id=1, source_target_pairs={{0,4},{4,8},{8,12},{12,16},{16,20},{20,24},{24,28},{1,5},{5,9},{9,... | collective-permute-start | bytes 196616 | tf_op jit(solution)/shard_map/while/body/eval_jaxpr/ppermute | solution.py:14
  80.0 4.4 %collective-permute-start = (bf16[2,2,64,128]{3,2,1,0:T(8,128)(2,1)S(1)}, bf16[2,2,64,128]{3,2,1,0:T(8,128)(2,1)S(1)}, u32[]{:S(2)}, u32[]{:S(2)}) collective-permute-start(bf16[2,2,64,128]{3,2,1,0:T(8,128)(2,1)S(1)} %get-tuple-element.3575), channel_id=1, source_target_pairs={{0,4},{4,8},{8,12},{12,16},{16,20},{20,24},{24,28},{1,5},{5,9},{9,... | collective-permute-start | bytes 196616 | tf_op jit(solution)/shard_map/while/body/eval_jaxpr/ppermute | solution.py:14
  86.3 7.8 %all-to-all-start.7 = ((bf16[8,16,1024]{2,1,0:T(8,128)(2,1)}), bf16[8,16,1024]{2,1,0:T(8,128)(2,1)S(1)}, u32[]{:S(2)}, u32[]{:S(2)}) async-start(bf16[8,16,1024]{2,1,0:T(8,128)(2,1)} %get-tuple-element.3061), calls=%async_computation.7 | async-start | bytes 524288 | tf_op jit(solution)/shard_map/all_to_all | solution.py:244
  94.2 13.3 %while.167 = (s32[]{:T(128)}, bf16[2,2,64,128]{3,2,1,0:T(8,128)(2,1)S(1)}, bf16[2,2,2,64,128]{4,3,2,1,0:T(8,128)(2,1)S(1)}, s32[]{:T(128)}) while((s32[]{:T(128)}, bf16[2,2,64,128]{3,2,1,0:T(8,128)(2,1)S(1)}, bf16[2,2,2,64,128]{4,3,2,1,0:T(8,128)(2,1)S(1)}, s32[]{:T(128)}) %tuple.449), condition=%wide.region_3.5_spmd, body=%wide.region_2.4_spmd.sunk | while | flops 2 | bytes 524393 | solution.py:63
  95.5 5.2 %collective-permute-done.1 = bf16[2,2,64,128]{3,2,1,0:T(8,128)(2,1)S(1)} collective-permute-done((bf16[2,2,64,128]{3,2,1,0:T(8,128)(2,1)S(1)}, bf16[2,2,64,128]{3,2,1,0:T(8,128)(2,1)S(1)}, u32[]{:S(2)}, u32[]{:S(2)}) %collective-permute-start.1) | collective-permute-done | bytes 65568 | tf_op jit(solution)/shard_map/while/body/eval_jaxpr/ppermute | solution.py:14
  102.1 5.4 %collective-permute-done.1 = bf16[2,2,64,128]{3,2,1,0:T(8,128)(2,1)S(1)} collective-permute-done((bf16[2,2,64,128]{3,2,1,0:T(8,128)(2,1)S(1)}, bf16[2,2,64,128]{3,2,1,0:T(8,128)(2,1)S(1)}, u32[]{:S(2)}, u32[]{:S(2)}) %collective-permute-start.1) | collective-permute-done | bytes 65568 | tf_op jit(solution)/shard_map/while/body/eval_jaxpr/ppermute | solution.py:14
  107.9 4.5 %while.170 = (s32[]{:T(128)}, f32[8,64]{1,0:T(8,128)S(1)}, f32[8,64]{1,0:T(8,128)S(1)}, s32[]{:T(128)}, s32[1024]{0:T(1024)S(1)}, /*index=5*/s32[64]{0:T(128)S(1...) while((s32[]{:T(128)}, f32[8,64]{1,0:T(8,128)S(1)}, ...), condition=%wide.region_9.12_spmd.clone, body=%wide.region_4.11_spmd.clone.sunk | while | flops 8565923 | bytes 451963 | solution.py:157
  112.5 4.6 %while.171 = (s32[]{:T(128)}, f32[8,64,128]{2,1,0:T(8,128)S(1)}, s32[]{:T(128)}, s32[1024]{0:T(1024)S(1)}, s32[64]{0:T(128)S(1)}, /*index=5*/bf16[5,2,2,64,128]{...) while((s32[]{:T(128)}, f32[8,64,128]{2,1,0:T(8,128)S(1)}, ...), condition=%wide.region_13.16_spmd.clone, body=%wide.region_10.15_spmd.clone.sunk | while | flops 16986276 | bytes 710495 | solution.py:174
  117.7 5.4 %while.174 = (s32[]{:T(128)}, f32[8,64,128]{2,1,0:T(8,128)S(1)}, f32[5,2,2,64,128]{4,3,2,1,0:T(8,128)S(1)}, s32[]{:T(128)}, s32[1024]{0:T(1024)S(1)}, /*index=5*...) while((s32[]{:T(128)}, f32[8,64,128]{2,1,0:T(8,128)S(1)}, ...), condition=%wide.region_28.31_spmd.clone, body=%wide.region_25.30_spmd.clone.sunk | while | flops 42356896 | bytes 2170323 | solution.py:215
  123.1 5.1 %while.172 = (s32[]{:T(128)}, f32[8,64]{1,0:T(8,128)S(1)}, f32[8,64]{1,0:T(8,128)S(1)}, s32[]{:T(128)}, s32[1024]{0:T(1024)S(1)}, /*index=5*/s32[64]{0:T(128)S(1...) while((s32[]{:T(128)}, f32[8,64]{1,0:T(8,128)S(1)}, ...), condition=%wide.region_19.22_spmd.clone, body=%wide.region_14.21_spmd.clone.sunk | while | flops 8565923 | bytes 451979 | solution.py:157
  128.3 5.3 %while.173 = (s32[]{:T(128)}, f32[8,64,128]{2,1,0:T(8,128)S(1)}, s32[]{:T(128)}, s32[1024]{0:T(1024)S(1)}, s32[64]{0:T(128)S(1)}, /*index=5*/s32[]{:T(128)}, bf1...) while((s32[]{:T(128)}, f32[8,64,128]{2,1,0:T(8,128)S(1)}, ...), condition=%wide.region_23.26_spmd.clone, body=%wide.region_20.25_spmd.clone.sunk | while | flops 16986276 | bytes 710511 | solution.py:174
  134.0 6.8 %while.175 = (s32[]{:T(128)}, f32[8,64,128]{2,1,0:T(8,128)S(1)}, f32[5,2,2,64,128]{4,3,2,1,0:T(8,128)S(1)}, s32[]{:T(128)}, s32[1024]{0:T(1024)S(1)}, /*index=5*...) while((s32[]{:T(128)}, f32[8,64,128]{2,1,0:T(8,128)S(1)}, ...), condition=%wide.region_33.36_spmd.clone, body=%wide.region_30.35_spmd.clone.sunk | while | flops 42356896 | bytes 2170339 | solution.py:215
  140.9 17.6 %while.169 = (s32[]{:T(128)}, f32[2,2,64,128]{3,2,1,0:T(8,128)S(1)}, f32[2,2,2,64,128]{4,3,2,1,0:T(8,128)S(1)}, s32[]{:T(128)}) while((s32[]{:T(128)}, f32[2,2,64,128]{3,2,1,0:T(8,128)S(1)}, f32[2,2,2,64,128]{4,3,2,1,0:T(8,128)S(1)}, s32[]{:T(128)}) %tuple.473), condition=%wide.region_37.40_spmd, body=%wide.region_36.39_spmd.sunk | while | flops 32770 | bytes 917601 | solution.py:83
  140.9 7.5 %collective-permute-start.3 = (f32[2,2,64,128]{3,2,1,0:T(8,128)S(1)}, f32[2,2,64,128]{3,2,1,0:T(8,128)S(1)}, u32[]{:S(2)}, u32[]{:S(2)}) collective-permute-start(f32[2,2,64,128]{3,2,1,0:T(8,128)S(1)} %bitcast_add_fusion.6), channel_id=1, source_target_pairs={{0,4},{4,8},{8,12},{12,16},{16,20},{20,24},{24,28},{1,5},{5,9},{9,... | collective-permute-start | bytes 393224 | tf_op jit(solution)/shard_map/while/body/eval_jaxpr/ppermute | solution.py:14
  151.6 4.4 %collective-permute-start.3 = (f32[2,2,64,128]{3,2,1,0:T(8,128)S(1)}, f32[2,2,64,128]{3,2,1,0:T(8,128)S(1)}, u32[]{:S(2)}, u32[]{:S(2)}) collective-permute-start(f32[2,2,64,128]{3,2,1,0:T(8,128)S(1)} %bitcast_add_fusion.6), channel_id=1, source_target_pairs={{0,4},{4,8},{8,12},{12,16},{16,20},{20,24},{24,28},{1,5},{5,9},{9,... | collective-permute-start | bytes 393224 | tf_op jit(solution)/shard_map/while/body/eval_jaxpr/ppermute | solution.py:14
  158.5 16.0 %while.168 = (s32[]{:T(128)}, f32[2,2,64,128]{3,2,1,0:T(8,128)S(1)}, f32[2,2,2,64,128]{4,3,2,1,0:T(8,128)S(1)}, s32[]{:T(128)}) while((s32[]{:T(128)}, f32[2,2,64,128]{3,2,1,0:T(8,128)S(1)}, f32[2,2,2,64,128]{4,3,2,1,0:T(8,128)S(1)}, s32[]{:T(128)}) %tuple.476), condition=%wide.region_35.38_spmd, body=%wide.region_34.37_spmd.sunk | while | flops 32770 | bytes 917601 | solution.py:73
  159.8 6.4 %collective-permute-done.2 = f32[2,2,64,128]{3,2,1,0:T(8,128)S(1)} collective-permute-done((f32[2,2,64,128]{3,2,1,0:T(8,128)S(1)}, f32[2,2,64,128]{3,2,1,0:T(8,128)S(1)}, u32[]{:S(2)}, u32[]{:S(2)}) %collective-permute-start.2) | collective-permute-done | bytes 131104 | tf_op jit(solution)/shard_map/while/body/eval_jaxpr/ppermute | solution.py:14
  167.6 6.9 %collective-permute-done.2 = f32[2,2,64,128]{3,2,1,0:T(8,128)S(1)} collective-permute-done((f32[2,2,64,128]{3,2,1,0:T(8,128)S(1)}, f32[2,2,64,128]{3,2,1,0:T(8,128)S(1)}, u32[]{:S(2)}, u32[]{:S(2)}) %collective-permute-start.2) | collective-permute-done | bytes 131104 | tf_op jit(solution)/shard_map/while/body/eval_jaxpr/ppermute | solution.py:14
  (201 shorter events, 48.9 us)
Async XLA Ops:
  0.6 14.0 %all-to-all-start = ((bf16[8,16,128]{2,1,0:T(8,128)(2,1)}), bf16[8,16,128]{2,1,0:T(8,128)(2,1)S(1)}, u32[]{:S(2)}, u32[]{:S(2)}) async-start(bf16[8,16,128]{2,1,0:T(8,128)(2,1)} %bitcast.338), calls=%async_computation | async-start | bytes 65536 | tf_op jit(solution)/shard_map/all_to_all | solution.py:239
  14.6 10.0 %all-to-all-start.2 = ((bf16[8,16,128]{2,1,0:T(8,128)(2,1)}), bf16[8,16,128]{2,1,0:T(8,128)(2,1)S(1)}, u32[]{:S(2)}, u32[]{:S(2)}) async-start(bf16[8,16,128]{2,1,0:T(8,128)(2,1)} %bitcast.47), calls=%async_computation.2 | async-start | bytes 65536 | tf_op jit(solution)/shard_map/all_to_all | solution.py:240
  25.8 10.0 %all-to-all-start.3 = ((bf16[8,16,128]{2,1,0:T(8,128)(2,1)}), bf16[8,16,128]{2,1,0:T(8,128)(2,1)S(1)}, u32[]{:S(2)}, u32[]{:S(2)}) async-start(bf16[8,16,128]{2,1,0:T(8,128)(2,1)} %get-tuple-element.3063), calls=%async_computation.3 | async-start | bytes 65536 | tf_op jit(solution)/shard_map/all_to_all | solution.py:246
  35.8 3.5 %copy-start = (s32[1024]{0:T(1024)S(1)}, s32[1024]{0:T(1024)}, u32[]{:S(2)}) copy-start(s32[1024]{0:T(1024)} %param.45) | copy-start | bytes 12292
  35.8 10.1 %all-to-all-start.1 = ((bf16[8,16,128]{2,1,0:T(8,128)(2,1)}), bf16[8,16,128]{2,1,0:T(8,128)(2,1)S(1)}, u32[]{:S(2)}, u32[]{:S(2)}) async-start(bf16[8,16,128]{2,1,0:T(8,128)(2,1)} %get-tuple-element.3062), calls=%async_computation.1 | async-start | bytes 65536 | tf_op jit(solution)/shard_map/all_to_all | solution.py:245
  45.9 11.6 %all-to-all-start.6 = ((bf16[8,16,1024]{2,1,0:T(8,128)(2,1)}), bf16[8,16,1024]{2,1,0:T(8,128)(2,1)S(1)}, u32[]{:S(2)}, u32[]{:S(2)}) async-start(bf16[8,16,1024]{2,1,0:T(8,128)(2,1)} %bitcast.59), calls=%async_computation.6 | async-start | bytes 524288 | tf_op jit(solution)/shard_map/all_to_all | solution.py:238
  57.5 11.6 %all-to-all-start.4 = ((bf16[8,16,1024]{2,1,0:T(8,128)(2,1)}), bf16[8,16,1024]{2,1,0:T(8,128)(2,1)S(1)}, u32[]{:S(2)}, u32[]{:S(2)}) async-start(bf16[8,16,1024]{2,1,0:T(8,128)(2,1)} %bitcast.53), calls=%async_computation.4 | async-start | bytes 524288 | tf_op jit(solution)/shard_map/all_to_all | solution.py:237
  70.5 15.8 %all-to-all-start.5 = ((bf16[8,16,1024]{2,1,0:T(8,128)(2,1)}), bf16[8,16,1024]{2,1,0:T(8,128)(2,1)S(1)}, u32[]{:S(2)}, u32[]{:S(2)}) async-start(bf16[8,16,1024]{2,1,0:T(8,128)(2,1)} %get-tuple-element.3060), calls=%async_computation.5 | async-start | bytes 524288 | tf_op jit(solution)/shard_map/all_to_all | solution.py:243
  74.0 5.9 %collective-permute-start = (bf16[2,2,64,128]{3,2,1,0:T(8,128)(2,1)S(1)}, bf16[2,2,64,128]{3,2,1,0:T(8,128)(2,1)S(1)}, u32[]{:S(2)}, u32[]{:S(2)}) collective-permute-start(bf16[2,2,64,128]{3,2,1,0:T(8,128)(2,1)S(1)} %get-tuple-element.3575), channel_id=1, source_target_pairs={{0,4},{4,8},{8,12},{12,16},{16,20},{20,24},{24,28},{1,5},{5,9},{9,... | collective-permute-start | bytes 196616 | tf_op jit(solution)/shard_map/while/body/eval_jaxpr/ppermute | solution.py:14
  80.0 6.3 %collective-permute-start = (bf16[2,2,64,128]{3,2,1,0:T(8,128)(2,1)S(1)}, bf16[2,2,64,128]{3,2,1,0:T(8,128)(2,1)S(1)}, u32[]{:S(2)}, u32[]{:S(2)}) collective-permute-start(bf16[2,2,64,128]{3,2,1,0:T(8,128)(2,1)S(1)} %get-tuple-element.3575), channel_id=1, source_target_pairs={{0,4},{4,8},{8,12},{12,16},{16,20},{20,24},{24,28},{1,5},{5,9},{9,... | collective-permute-start | bytes 196616 | tf_op jit(solution)/shard_map/while/body/eval_jaxpr/ppermute | solution.py:14
  86.3 21.3 %all-to-all-start.7 = ((bf16[8,16,1024]{2,1,0:T(8,128)(2,1)}), bf16[8,16,1024]{2,1,0:T(8,128)(2,1)S(1)}, u32[]{:S(2)}, u32[]{:S(2)}) async-start(bf16[8,16,1024]{2,1,0:T(8,128)(2,1)} %get-tuple-element.3061), calls=%async_computation.7 | async-start | bytes 524288 | tf_op jit(solution)/shard_map/all_to_all | solution.py:244
  94.2 6.5 %collective-permute-start.1 = (bf16[2,2,64,128]{3,2,1,0:T(8,128)(2,1)S(1)}, bf16[2,2,64,128]{3,2,1,0:T(8,128)(2,1)S(1)}, u32[]{:S(2)}, u32[]{:S(2)}) collective-permute-start(bf16[2,2,64,128]{3,2,1,0:T(8,128)(2,1)S(1)} %get-tuple-element.3563), channel_id=1, source_target_pairs={{4,0},{8,4},{12,8},{16,12},{20,16},{24,20},{28,24},{5,1},{9,5},{13... | collective-permute-start | bytes 196616 | tf_op jit(solution)/shard_map/while/body/eval_jaxpr/ppermute | solution.py:14
  100.8 6.7 %collective-permute-start.1 = (bf16[2,2,64,128]{3,2,1,0:T(8,128)(2,1)S(1)}, bf16[2,2,64,128]{3,2,1,0:T(8,128)(2,1)S(1)}, u32[]{:S(2)}, u32[]{:S(2)}) collective-permute-start(bf16[2,2,64,128]{3,2,1,0:T(8,128)(2,1)S(1)} %get-tuple-element.3563), channel_id=1, source_target_pairs={{4,0},{8,4},{12,8},{16,12},{20,16},{24,20},{28,24},{5,1},{9,5},{13... | collective-permute-start | bytes 196616 | tf_op jit(solution)/shard_map/while/body/eval_jaxpr/ppermute | solution.py:14
  140.9 10.6 %collective-permute-start.3 = (f32[2,2,64,128]{3,2,1,0:T(8,128)S(1)}, f32[2,2,64,128]{3,2,1,0:T(8,128)S(1)}, u32[]{:S(2)}, u32[]{:S(2)}) collective-permute-start(f32[2,2,64,128]{3,2,1,0:T(8,128)S(1)} %bitcast_add_fusion.6), channel_id=1, source_target_pairs={{0,4},{4,8},{8,12},{12,16},{16,20},{20,24},{24,28},{1,5},{5,9},{9,... | collective-permute-start | bytes 393224 | tf_op jit(solution)/shard_map/while/body/eval_jaxpr/ppermute | solution.py:14
  151.6 6.9 %collective-permute-start.3 = (f32[2,2,64,128]{3,2,1,0:T(8,128)S(1)}, f32[2,2,64,128]{3,2,1,0:T(8,128)S(1)}, u32[]{:S(2)}, u32[]{:S(2)}) collective-permute-start(f32[2,2,64,128]{3,2,1,0:T(8,128)S(1)} %bitcast_add_fusion.6), channel_id=1, source_target_pairs={{0,4},{4,8},{8,12},{12,16},{16,20},{20,24},{24,28},{1,5},{5,9},{9,... | collective-permute-start | bytes 393224 | tf_op jit(solution)/shard_map/while/body/eval_jaxpr/ppermute | solution.py:14
  158.5 7.7 %collective-permute-start.2 = (f32[2,2,64,128]{3,2,1,0:T(8,128)S(1)}, f32[2,2,64,128]{3,2,1,0:T(8,128)S(1)}, u32[]{:S(2)}, u32[]{:S(2)}) collective-permute-start(f32[2,2,64,128]{3,2,1,0:T(8,128)S(1)} %bitcast_add_fusion.5), channel_id=1, source_target_pairs={{4,0},{8,4},{12,8},{16,12},{20,16},{24,20},{28,24},{5,1},{9,5},{13... | collective-permute-start | bytes 393224 | tf_op jit(solution)/shard_map/while/body/eval_jaxpr/ppermute | solution.py:14
  166.3 8.2 %collective-permute-start.2 = (f32[2,2,64,128]{3,2,1,0:T(8,128)S(1)}, f32[2,2,64,128]{3,2,1,0:T(8,128)S(1)}, u32[]{:S(2)}, u32[]{:S(2)}) collective-permute-start(f32[2,2,64,128]{3,2,1,0:T(8,128)S(1)} %bitcast_add_fusion.5), channel_id=1, source_target_pairs={{4,0},{8,4},{12,8},{16,12},{20,16},{24,20},{28,24},{5,1},{9,5},{13... | collective-permute-start | bytes 393224 | tf_op jit(solution)/shard_map/while/body/eval_jaxpr/ppermute | solution.py:14
where the time goes:
time: 179 us; the launch traced here: 177 us
  waiting for transfers between devices  75.1 us (42%)
  starting transfers between devices  60.8 us (34%)
  local copies, waits for them, and re-layouts  15.1 us (8%)
  loops' own time  13.9 us (8%)
  matrix products  5.67 us (3%)
  other arithmetic  5.09 us (3%)
    ppermute x8, waiting for transfers between devices, shifted(): return lax.ppermute(block, axis, route)  33.6 us
    ppermute x8, starting transfers between devices, shifted(): return lax.ppermute(block, axis, route)  25.3 us
    all_to_all x2, waiting for transfers between devices, shards(): lax.all_to_all(arranged[2], 'ctx', split_axis=0, concat_axis=0, tiled=True)  13.2 us
    all_to_all x2, waiting for transfers between devices, shards(): lax.all_to_all(arranged[3], 'ctx', split_axis=0, concat_axis=0, tiled=True)  12.6 us
    all_to_all x2, starting transfers between devices, shards(): lax.all_to_all(arranged[1], 'ctx', split_axis=0, concat_axis=0, tiled=True)  11.3 us
    all_to_all x2, starting transfers between devices, shards(): lax.all_to_all(arranged[2], 'ctx', split_axis=0, concat_axis=0, tiled=True)  10.7 us
    dynamic_slice x18, local copies, waits for them, and re-layouts, tile_needed(): lax.dynamic_slice_in_dim(doc_all, safe_stretch * stretch_rows + stretch_r...  10.6 us
    all_to_all x2, waiting for transfers between devices, shards(): lax.all_to_all(arranged[1], 'ctx', split_axis=0, concat_axis=0, tiled=True)  8.13 us
  transfers between devices with their start and end apart: 16, of which 14 were waited for; matrix products, arithmetic and copies ran while one was open for 1% of the time, Pallas kernels for 0%

commit v1 on v0

v1 whole, which is shorter than its diff:
```python
import functools
import math

import jax
import jax.numpy as jnp
from jax import lax
from jax.experimental import pallas as pl
from jax.experimental.pallas import tpu as pltpu
from jax.sharding import PartitionSpec as P

NEG_FILL = -1e30
LANES = 128
GROUP_HEADS = 2
MESH = pl.DeviceIdType.MESH


def kernel(
    members,
    halo,
    q_ref,
    k_ref,
    v_ref,
    g_ref,
    doc_ref,
    out_ref,
    dq_ref,
    dk_ref,
    dv_ref,
    window,
    out_stage,
    dq_stage,
    term_stage,
    term_in,
    kv_send,
    kv_recv,
    row_send,
    row_recv,
    term_send,
    term_recv,
):
    me = lax.axis_index("ctx")
    rows, width = q_ref.shape
    head_dim = k_ref.shape[1]
    heads = width // head_dim
    half_rows = rows // 2
    scaling = 1.0 / math.sqrt(head_dim)
    groups = heads // GROUP_HEADS
    keys = (halo + 1) * rows

    def place(block):
        upper = block >= members
        return jnp.where(upper, 2 * members - 1 - block, block), upper.astype(jnp.int32)

    def remote(src, dst, send, recv, target):
        return pltpu.make_async_remote_copy(
            src_ref=src,
            dst_ref=dst,
            send_sem=send,
            recv_sem=recv,
            device_id={"ctx": target},
            device_id_type=MESH,
        )

    sources = (me // 2, (2 * members - 1 - me) // 2)
    barrier = pltpu.get_barrier_semaphore()

    def greet(device):
        pl.semaphore_signal(barrier, inc=1, device_id={"ctx": device}, device_id_type=MESH)

    expected = jnp.int32(0)
    for j in range(1, halo + 1):
        pl.when(me - j >= 0)(functools.partial(greet, me - j))
        expected += (me + j < members).astype(jnp.int32)
    for j in range(halo + 1):
        for slot in range(2):
            source = sources[slot] + j
            pl.when((source < members) & (source != me))(functools.partial(greet, source))
        for half in range(2):
            target, _ = place(2 * (me - j) + half)
            expected += ((me - j >= 0) & (target != me)).astype(jnp.int32)
    pl.semaphore_wait(barrier, expected)

    def kv_copies(j, target):
        return [
            remote(ref, window.at[j - 1, i], kv_send.at[j - 1, i], kv_recv.at[j - 1, i], target)
            for i, ref in enumerate((k_ref, v_ref))
        ]

    for j in range(1, halo + 1):

        @pl.when(me + j < members)
        def _():
            for copy in kv_copies(j, me + j):
                copy.start()

    per_chunk = rows // LANES
    query_doc = jnp.concatenate(
        [doc_ref[pl.ds(me * per_chunk + i, 1), :] for i in range(per_chunk)], axis=1
    )
    columns = []
    for j in range(halo, -1, -1):
        chunk = me - j
        safe = jnp.maximum(chunk, 0)
        for i in range(per_chunk):
            row = doc_ref[pl.ds(safe * per_chunk + i, 1), :]
            column = jnp.broadcast_to(row, (LANES, LANES)).T
            columns.append(jnp.where(chunk >= 0, column, -1))
    key_doc = jnp.concatenate(columns, axis=0)
    key_doc = jnp.concatenate([key_doc] * per_chunk, axis=1)
    key_pos = lax.broadcasted_iota(jnp.int32, (keys, rows), 0) - halo * rows
    query_pos = lax.broadcasted_iota(jnp.int32, (keys, rows), 1)
    allowed = (key_doc == query_doc) & (key_pos <= query_pos)
    bias = jnp.where(allowed, 0.0, NEG_FILL)

    for j in range(1, halo + 1):

        @pl.when(me - j >= 0)
        def _():
            for copy in kv_copies(j, me):
                copy.wait_recv()

        @pl.when(me - j < 0)
        def _():
            window[j - 1] = jnp.zeros(window.shape[1:], window.dtype)

    key_win = jnp.concatenate([window[j - 1, 0] for j in range(halo, 0, -1)] + [k_ref[...]], axis=0)
    value_win = jnp.concatenate(
        [window[j - 1, 1] for j in range(halo, 0, -1)] + [v_ref[...]], axis=0
    )

    def dot(a, b, contract):
        return lax.dot_general(
            a, b, (((contract[0],), (contract[1],)), ((), ())), preferred_element_type=jnp.float32
        )

    def head(h, totals):
        key_acc, value_acc = totals
        at = pl.ds(pl.multiple_of(h * head_dim, head_dim), head_dim)
        q_head = q_ref[:, at]
        g_head = g_ref[:, at]
        scores = dot(key_win, q_head, (1, 1)) + bias
        top = jnp.max(scores, axis=0, keepdims=True)
        raised = jnp.exp2((scores - top) * (scaling * math.log2(math.e)))
        weights = raised * (1.0 / jnp.sum(raised, axis=0, keepdims=True))
        probs = weights.astype(jnp.bfloat16)
        dprobs = dot(value_win, g_head, (1, 1))
        row_dot = jnp.sum(weights * dprobs, axis=0, keepdims=True)
        dscores = (weights * (dprobs - row_dot)).astype(jnp.bfloat16)
        out_stage[:, at] = dot(probs, value_win, (0, 0)).astype(jnp.bfloat16)
        dq_stage[:, at] = (scaling * dot(dscores, key_win, (0, 0))).astype(jnp.bfloat16)
        return (key_acc + dot(dscores, q_head, (1, 0)), value_acc + dot(probs, g_head, (1, 0)))

    def row_copies(group, half, finish):
        target, slot = place(2 * me + half)
        at = pl.ds(group * GROUP_HEADS * head_dim, GROUP_HEADS * head_dim)
        here = pl.ds(half * half_rows, half_rows)
        there = pl.ds(pl.multiple_of(slot * half_rows, half_rows), half_rows)
        for i, (stage, result) in enumerate(((out_stage, out_ref), (dq_stage, dq_ref))):
            src, dst = stage.at[here, at], result.at[there, at]
            send, recv = row_send.at[group, half, i], row_recv.at[group, slot, i]
            yield src, dst, send, recv, target

    def term_copy(j, half):
        target, slot = place(2 * (me - j) + half)
        return (
            term_stage.at[j, half],
            term_in.at[slot, j],
            term_send.at[j, half],
            term_recv.at[slot, j],
            target,
        )

    def start(src, dst, send, recv, target):
        @pl.when(target != me)
        def _():
            remote(src, dst, send, recv, target).start()

        @pl.when(target == me)
        def _():
            pltpu.make_async_copy(src, dst, recv).start()

    def finish_send(src, dst, send, recv, target):
        @pl.when(target != me)
        def _():
            remote(src, dst, send, recv, target).wait_send()

    totals = (jnp.zeros((keys, head_dim), jnp.float32),) * 2
    for group in range(groups):
        first = group * GROUP_HEADS
        if rows * keys <= 256 * 256:
            for h in range(first, first + GROUP_HEADS):
                totals = head(h, totals)
        else:
            totals = lax.fori_loop(first, first + GROUP_HEADS, head, totals)
        for half in range(2):
            for copy in row_copies(group, half, False):
                start(*copy)

    for i, total in enumerate((totals[0] * scaling, totals[1])):
        total = total.astype(jnp.bfloat16)
        for j in range(halo + 1):
            for half in range(2):
                low = (halo - j) * rows + half * half_rows
                term_stage[j, half, i] = total[low : low + half_rows]
    for j in range(halo, -1, -1):

        @pl.when(me - j >= 0)
        def _():
            for half in range(2):
                start(*term_copy(j, half))

    for group in range(groups):
        at = pl.ds(group * GROUP_HEADS * head_dim, GROUP_HEADS * head_dim)
        for slot in range(2):
            there = pl.ds(slot * half_rows, half_rows)
            for i, (stage, result) in enumerate(((out_stage, out_ref), (dq_stage, dq_ref))):
                pltpu.make_async_copy(
                    stage.at[there, at], result.at[there, at], row_recv.at[group, slot, i]
                ).wait()
    for slot in range(2):
        for j in range(halo + 1):

            @pl.when(sources[slot] + j < members)
            def _():
                pltpu.make_async_copy(
                    term_stage.at[j, slot], term_in.at[slot, j], term_recv.at[slot, j]
                ).wait()

            @pl.when(sources[slot] + j >= members)
            def _():
                term_in[slot, j] = jnp.zeros(term_in.shape[2:], term_in.dtype)

        there = pl.ds(slot * half_rows, half_rows)
        for i, result in enumerate((dk_ref, dv_ref)):
            total = term_in[slot, 0, i].astype(jnp.float32)
            for j in range(1, halo + 1):
                total += term_in[slot, j, i].astype(jnp.float32)
            result[there, :] = total

    for j in range(1, halo + 1):

        @pl.when(me + j < members)
        def _():
            for copy in kv_copies(j, me + j):
                copy.wait_send()

    for group in range(groups):
        for half in range(2):
            for copy in row_copies(group, half, True):
                finish_send(*copy)
    for j in range(halo + 1):

        @pl.when(me - j >= 0)
        def _():
            for half in range(2):
                finish_send(*term_copy(j, half))


def shards(queries, key_states, value_states, out_grad, doc_ids):
    members = lax.axis_size("ctx")
    rows, width = queries.shape
    head_dim = key_states.shape[1]
    half_rows = rows // 2
    halo = -(-(members // 4) * half_rows // rows)
    groups = width // head_dim // GROUP_HEADS
    docs = doc_ids.reshape(doc_ids.shape[0] // LANES, LANES)
    vmem = pl.BlockSpec(memory_space=pltpu.VMEM)
    hbm = pl.BlockSpec(memory_space=pl.ANY)
    dma = pltpu.SemaphoreType.DMA
    keys = (halo + 1) * rows
    return pl.pallas_call(
        functools.partial(kernel, members, halo),
        out_shape=(
            jax.ShapeDtypeStruct((rows, width), jnp.bfloat16),
            jax.ShapeDtypeStruct((rows, width), jnp.bfloat16),
            jax.ShapeDtypeStruct((rows, head_dim), jnp.float32),
            jax.ShapeDtypeStruct((rows, head_dim), jnp.float32),
        ),
        in_specs=[vmem] * 5,
        out_specs=(hbm, hbm, vmem, vmem),
        scratch_shapes=[
            pltpu.VMEM((halo, 2, rows, head_dim), jnp.bfloat16),
            pltpu.VMEM((rows, width), jnp.bfloat16),
            pltpu.VMEM((rows, width), jnp.bfloat16),
            pltpu.VMEM((halo + 1, 2, 2, half_rows, head_dim), jnp.bfloat16),
            pltpu.VMEM((2, halo + 1, 2, half_rows, head_dim), jnp.bfloat16),
            dma((halo, 2)),
            dma((halo, 2)),
            dma((groups, 2, 2)),
            dma((groups, 2, 2)),
            dma((halo + 1, 2)),
            dma((2, halo + 1)),
        ],
        compiler_params=pltpu.CompilerParams(
            collective_id=0, has_side_effects=True, vmem_limit_bytes=40 * 1024 * 1024
        ),
        cost_estimate=pl.CostEstimate(
            flops=12 * rows * keys * width,
            bytes_accessed=8 * rows * width + 12 * rows * head_dim,
            transcendentals=rows * keys * width // head_dim,
        ),
    )(queries, key_states, value_states, out_grad, docs)


def solution(mesh):
    placed = P(("grp", "ctx"), None)
    return jax.shard_map(
        shards,
        mesh=mesh,
        in_specs=(placed, placed, placed, placed, P("grp")),
        out_specs=(placed,) * 4,
        check_vma=False,
    )
```

time: 179 us -> 32.9 us (0.18); the launches traced: 177 us -> 32.5 us
  waiting for transfers between devices: 75.1 us -> 0 us
  starting transfers between devices: 60.8 us -> 0 us
  Pallas kernels: 0 us -> 25.1 us
  loops' own time: 13.9 us -> 0 us
  local copies, waits for them, and re-layouts: 15.1 us -> 6.76 us
  matrix products: 5.67 us -> 0 us
  other arithmetic: 5.09 us -> 0 us
    all_to_all x8 -> x0, waiting for transfers between devices: 41.5 us -> none  [the longest x2 13.2 us: shards(): lax.all_to_all(arranged[2], 'ctx', split_axis=0, concat_axis=0, tiled=True)]
    all_to_all x8 -> x0, starting transfers between devices: 35.5 us -> none  [the longest x2 11.3 us: shards(): lax.all_to_all(arranged[1], 'ctx', split_axis=0, concat_axis=0, tiled=True)]
    ppermute x8 -> x0, waiting for transfers between devices: 33.6 us -> none  [shifted(): return lax.ppermute(block, axis, route)]
    ppermute x8 -> x0, starting transfers between devices: 25.3 us -> none  [shifted(): return lax.ppermute(block, axis, route)]
    pallas_call x0 -> x1, Pallas kernels: none -> 25.1 us  [shards(): pl.pallas_call(functools.partial(kernel, members, halo), out_shape=(jax.S...]
    another operation x28 -> x0, loops' own time: 13.9 us -> none  [the longest x2 4.27 us: attend(): lax.fori_loop(0, reach_stretches + 1, back_step, (out_zero, grad_window))]
    dynamic_slice x28 -> x0, local copies, waits for them, and re-layouts: 11.3 us -> none  [the longest x18 10.6 us: tile_needed(): lax.dynamic_slice_in_dim(doc_all, safe_stretch * stretch_rows + stretch_r...]
    unnamed x11 -> x14, local copies, waits for them, and re-layouts: 0.31 us -> 6.76 us
  transfers between devices with their start and end apart: 16 -> 0, of which waited for: 14 -> 0; matrix products, arithmetic and copies ran while one was open for 1% -> 0% of each run, Pallas kernels for 0% -> 0%
where the time goes in v1:
time: 32.9 us; the launch traced here: 32.5 us
  Pallas kernels  25.1 us (76%)
  local copies, waits for them, and re-layouts  6.76 us (21%)
  between operations  0.65 us (2%)
    pallas_call x1, Pallas kernels, shards(): pl.pallas_call(functools.partial(kernel, members, halo), out_shape=(jax.S...  25.1 us
    unnamed x14, local copies, waits for them, and re-layouts  6.76 us

profile of v1, /device:TPU:0, one launch (start us, length us, event | category | flops | bytes accessed | tf_op | source)
XLA Modules:
  0.0 32.5 jit_solution(17643648711530468489)
XLA Ops:
  0.6 0.0 copy-start
  0.6 0.9 %copy-done = bf16[128,1024]{1,0:T(8,128)(2,1)S(1)} copy-done((bf16[128,1024]{1,0:T(8,128)(2,1)S(1)}, bf16[128,1024]{1,0:T(8,128)(2,1)}, u32[]{:S(2)}) %copy-start) | copy-done | bytes 262168
  1.6 0.0 copy-start.1
  1.6 0.9 %copy-done.1 = bf16[128,1024]{1,0:T(8,128)(2,1)S(1)} copy-done((bf16[128,1024]{1,0:T(8,128)(2,1)S(1)}, bf16[128,1024]{1,0:T(8,128)(2,1)}, u32[]{:S(2)}) %copy-start.1) | copy-done | bytes 262168
  2.5 0.0 copy-start.2
  2.5 0.8 %copy-done.2 = bf16[128,128]{1,0:T(8,128)(2,1)S(1)} copy-done((bf16[128,128]{1,0:T(8,128)(2,1)S(1)}, bf16[128,128]{1,0:T(8,128)(2,1)}, u32[]{:S(2)}) %copy-start.2) | copy-done | bytes 32792
  3.3 0.0 copy-start.3
  3.3 0.8 %copy-done.3 = bf16[128,128]{1,0:T(8,128)(2,1)S(1)} copy-done((bf16[128,128]{1,0:T(8,128)(2,1)S(1)}, bf16[128,128]{1,0:T(8,128)(2,1)}, u32[]{:S(2)}) %copy-start.3) | copy-done | bytes 32792
  4.1 0.0 copy-start.4
  4.1 0.7 %copy-done.4 = s32[1024]{0:T(1024)S(1)} copy-done((s32[1024]{0:T(1024)S(1)}, s32[1024]{0:T(1024)}, u32[]{:S(2)}) %copy-start.4) | copy-done | bytes 4120
  4.7 25.1 %shard_map.84 = (bf16[128,1024]{1,0:T(8,128)(2,1)S(1)}, bf16[128,1024]{1,0:T(8,128)(2,1)S(1)}, f32[128,128]{1,0:T(8,128)S(1)}, f32[128,128]{1,0:T(8,128)S(1)}) custom-call(bf16[128,1024]{1,0:T(8,128)(2,1)S(1)} %copy-done, bf16[128,128]{1,0:T(8,128)(2,1)S(1)} %copy-done.2, bf16[128,128]{1,0:T(8,128)(2,1)S(1)} %copy-done.3, bf16[128,1024]{1,0:T(8,128)(2,1)S(1)} %copy-done.1, ...), custom_call_target="tpu_custom_call" | custom-call | flops 402653184 | bytes 1245184 | tf_op jit(solution)/shard_map/pallas_call | solution.py:271
  29.9 0.7 %copy.13 = bf16[128,1024]{1,0:T(8,128)(2,1)} copy(bf16[128,1024]{1,0:T(8,128)(2,1)S(1)} %get-tuple-element.8) | data formatting | bytes 524288
  30.6 0.7 %copy.14 = bf16[128,1024]{1,0:T(8,128)(2,1)} copy(bf16[128,1024]{1,0:T(8,128)(2,1)S(1)} %get-tuple-element.9) | data formatting | bytes 524288
  31.3 0.6 %copy.15 = f32[128,128]{1,0:T(8,128)} copy(f32[128,128]{1,0:T(8,128)S(1)} %get-tuple-element.10) | data formatting | bytes 131072
  31.9 0.6 %copy.16 = f32[128,128]{1,0:T(8,128)} copy(f32[128,128]{1,0:T(8,128)S(1)} %get-tuple-element.11) | data formatting | bytes 131072
Async XLA Ops:
  0.6 1.0 %copy-start = (bf16[128,1024]{1,0:T(8,128)(2,1)S(1)}, bf16[128,1024]{1,0:T(8,128)(2,1)}, u32[]{:S(2)}) copy-start(bf16[128,1024]{1,0:T(8,128)(2,1)} %q_ref.1) | copy-start | bytes 786436
  1.6 0.9 %copy-start.1 = (bf16[128,1024]{1,0:T(8,128)(2,1)S(1)}, bf16[128,1024]{1,0:T(8,128)(2,1)}, u32[]{:S(2)}) copy-start(bf16[128,1024]{1,0:T(8,128)(2,1)} %g_ref.1) | copy-start | bytes 786436
  2.5 0.8 %copy-start.2 = (bf16[128,128]{1,0:T(8,128)(2,1)S(1)}, bf16[128,128]{1,0:T(8,128)(2,1)}, u32[]{:S(2)}) copy-start(bf16[128,128]{1,0:T(8,128)(2,1)} %k_ref.1) | copy-start | bytes 98308
  3.3 0.8 %copy-start.3 = (bf16[128,128]{1,0:T(8,128)(2,1)S(1)}, bf16[128,128]{1,0:T(8,128)(2,1)}, u32[]{:S(2)}) copy-start(bf16[128,128]{1,0:T(8,128)(2,1)} %v_ref.1) | copy-start | bytes 98308
  4.1 0.7 %copy-start.4 = (s32[1024]{0:T(1024)S(1)}, s32[1024]{0:T(1024)}, u32[]{:S(2)}) copy-start(s32[1024]{0:T(1024)} %param.9) | copy-start | bytes 12292

commit v2 on v1

--- a/solution.py
+++ b/solution.py
@@ -17,20 +17,24 @@
 def kernel(
     members,
     halo,
+    q_hbm,
+    k_hbm,
+    v_hbm,
+    g_hbm,
+    doc_hbm,
+    out_ref,
+    dq_ref,
+    term_in,
     q_ref,
     k_ref,
     v_ref,
     g_ref,
     doc_ref,
-    out_ref,
-    dq_ref,
-    dk_ref,
-    dv_ref,
     window,
     out_stage,
     dq_stage,
     term_stage,
-    term_in,
+    load_sem,
     kv_send,
     kv_recv,
     row_send,
@@ -47,6 +51,21 @@
     groups = heads // GROUP_HEADS
     keys = (halo + 1) * rows
 
+    loads = [
+        pltpu.make_async_copy(src, dst, load_sem.at[i])
+        for i, (src, dst) in enumerate(
+            (
+                (doc_hbm, doc_ref),
+                (k_hbm, k_ref),
+                (v_hbm, v_ref),
+                (q_hbm, q_ref),
+                (g_hbm, g_ref),
+            )
+        )
+    ]
+    for load in loads:
+        load.start()
+
     def place(block):
         upper = block >= members
         return jnp.where(upper, 2 * members - 1 - block, block), upper.astype(jnp.int32)
@@ -83,7 +102,7 @@
     def kv_copies(j, target):
         return [
             remote(ref, window.at[j - 1, i], kv_send.at[j - 1, i], kv_recv.at[j - 1, i], target)
-            for i, ref in enumerate((k_ref, v_ref))
+            for i, ref in enumerate((k_hbm, v_hbm))
         ]
 
     for j in range(1, halo + 1):
@@ -92,6 +111,8 @@
         def _():
             for copy in kv_copies(j, me + j):
                 copy.start()
+
+    loads[0].wait()
 
     per_chunk = rows // LANES
     query_doc = jnp.concatenate(
@@ -112,6 +133,8 @@
     allowed = (key_doc == query_doc) & (key_pos <= query_pos)
     bias = jnp.where(allowed, 0.0, NEG_FILL)
 
+    for load in loads[1:]:
+        load.wait()
     for j in range(1, halo + 1):
 
         @pl.when(me - j >= 0)
@@ -230,13 +253,6 @@
             def _():
                 term_in[slot, j] = jnp.zeros(term_in.shape[2:], term_in.dtype)
 
-        there = pl.ds(slot * half_rows, half_rows)
-        for i, result in enumerate((dk_ref, dv_ref)):
-            total = term_in[slot, 0, i].astype(jnp.float32)
-            for j in range(1, halo + 1):
-                total += term_in[slot, j, i].astype(jnp.float32)
-            result[there, :] = total
-
     for j in range(1, halo + 1):
 
         @pl.when(me + j < members)
@@ -254,6 +270,27 @@
         def _():
             for half in range(2):
                 finish_send(*term_copy(j, half))
+
+
+def finish(out_in, dq_in, terms, out_ref, dq_ref, dk_ref, dv_ref, grads, sems):
+    rows = [
+        pltpu.make_async_copy(out_in, out_ref, sems.at[0]),
+        pltpu.make_async_copy(dq_in, dq_ref, sems.at[1]),
+    ]
+    for copy in rows:
+        copy.start()
+    half_rows = terms.shape[3]
+    for i, result in enumerate((dk_ref, dv_ref)):
+        for slot in range(2):
+            total = terms[slot, 0, i].astype(jnp.float32)
+            for j in range(1, terms.shape[1]):
+                total += terms[slot, j, i].astype(jnp.float32)
+            grads[i, pl.ds(slot * half_rows, half_rows), :] = total
+        copy = pltpu.make_async_copy(grads.at[i], result, sems.at[2 + i])
+        copy.start()
+        rows.append(copy)
+    for copy in rows:
+        copy.wait()
 
 
 def shards(queries, key_states, value_states, out_grad, doc_ids):
@@ -265,25 +302,33 @@
     groups = width // head_dim // GROUP_HEADS
     docs = doc_ids.reshape(doc_ids.shape[0] // LANES, LANES)
     vmem = pl.BlockSpec(memory_space=pltpu.VMEM)
-    hbm = pl.BlockSpec(memory_space=pl.ANY)
+    hbm = pl.BlockSpec(memory_space=pltpu.HBM)
+    anywhere = pl.BlockSpec(memory_space=pl.ANY)
     dma = pltpu.SemaphoreType.DMA
     keys = (halo + 1) * rows
-    return pl.pallas_call(
+    row_shape = jax.ShapeDtypeStruct((rows, width), jnp.bfloat16)
+    grad_shape = jax.ShapeDtypeStruct((rows, head_dim), jnp.float32)
+    operands = (queries, key_states, value_states, out_grad, docs)
+    out_rows, dq_rows, terms = pl.pallas_call(
         functools.partial(kernel, members, halo),
         out_shape=(
-            jax.ShapeDtypeStruct((rows, width), jnp.bfloat16),
-            jax.ShapeDtypeStruct((rows, width), jnp.bfloat16),
-            jax.ShapeDtypeStruct((rows, head_dim), jnp.float32),
-            jax.ShapeDtypeStruct((rows, head_dim), jnp.float32),
+            row_shape,
+            row_shape,
+            jax.ShapeDtypeStruct((2, halo + 1, 2, half_rows, head_dim), jnp.bfloat16),
         ),
-        in_specs=[vmem] * 5,
-        out_specs=(hbm, hbm, vmem, vmem),
+        in_specs=[hbm] * 5,
+        out_specs=(vmem, vmem, vmem),
         scratch_shapes=[
+            pltpu.VMEM((rows, width), jnp.bfloat16),
+            pltpu.VMEM((rows, head_dim), jnp.bfloat16),
+            pltpu.VMEM((rows, head_dim), jnp.bfloat16),
+            pltpu.VMEM((rows, width), jnp.bfloat16),
+            pltpu.VMEM(docs.shape, jnp.int32),
             pltpu.VMEM((halo, 2, rows, head_dim), jnp.bfloat16),
             pltpu.VMEM((rows, width), jnp.bfloat16),
             pltpu.VMEM((rows, width), jnp.bfloat16),
             pltpu.VMEM((halo + 1, 2, 2, half_rows, head_dim), jnp.bfloat16),
-            pltpu.VMEM((2, halo + 1, 2, half_rows, head_dim), jnp.bfloat16),
+            dma((5,)),
             dma((halo, 2)),
             dma((halo, 2)),
             dma((groups, 2, 2)),
@@ -299,7 +344,15 @@
             bytes_accessed=8 * rows * width + 12 * rows * head_dim,
             transcendentals=rows * keys * width // head_dim,
         ),
-    )(queries, key_states, value_states, out_grad, docs)
+    )(*(pltpu.with_memory_space_constraint(x, pltpu.HBM) for x in operands))
+    return pl.pallas_call(
+        finish,
+        out_shape=(row_shape, row_shape, grad_shape, grad_shape),
+        in_specs=[anywhere, anywhere, vmem],
+        out_specs=(hbm,) * 4,
+        scratch_shapes=[pltpu.VMEM((2, rows, head_dim), jnp.float32), dma((4,))],
+        compiler_params=pltpu.CompilerParams(vmem_limit_bytes=16 * 1024 * 1024),
+    )(out_rows, dq_rows, terms)
 
 
 def solution(mesh):

time: 32.9 us -> 27 us (0.82)
  local copies, waits for them, and re-layouts: 6.76 us -> 0 us
  Pallas kernels: 25.1 us -> 26.3 us
    unnamed x14 -> x0, local copies, waits for them, and re-layouts: 6.76 us -> none
    pallas_call x1 -> x2, Pallas kernels: 25.1 us -> 26.3 us  [the longest x1 25.4 us: shards(): pl.pallas_call(functools.partial(kernel, members, halo), out_shape=(row_s...]
where the time goes in v2:
time: 27 us; the launch traced here: 26.9 us
  Pallas kernels  26.3 us (97%)
  between operations  0.64 us (2%)
    pallas_call x1, Pallas kernels, shards(): pl.pallas_call(functools.partial(kernel, members, halo), out_shape=(row_s...  25.4 us
    pallas_call x1, Pallas kernels, shards(): pl.pallas_call(finish, out_shape=(row_shape, row_shape, grad_shape, grad_...  0.86 us

profile of v2, /device:TPU:0, one launch (start us, length us, event | category | flops | bytes accessed | tf_op | source)
XLA Modules:
  0.0 26.9 jit_solution(14987192579165145300)
XLA Ops:
  0.6 25.4 %shard_map.84 = (bf16[128,1024]{1,0:T(8,128)(2,1)S(1)}, bf16[128,1024]{1,0:T(8,128)(2,1)S(1)}, bf16[2,2,2,64,128]{4,3,2,1,0:T(8,128)(2,1)S(1)}) custom-call(bf16[128,1024]{1,0:T(8,128)(2,1)} %q_hbm.1, bf16[128,128]{1,0:T(8,128)(2,1)} %k_hbm.1, bf16[128,128]{1,0:T(8,128)(2,1)} %v_hbm.1, bf16[128,1024]{1,0:T(8,128)(2,1)} %g_hbm.1, s32[8,128]{1,0:T(8,128)} %bitcast.1), custom_call_target="tpu_custom_call" | custom-call | flops 402653184 | bytes 1245184 | tf_op jit(solution)/shard_map/pallas_call | solution.py:312
  26.0 0.9 %shard_map.85 = (bf16[128,1024]{1,0:T(8,128)(2,1)}, bf16[128,1024]{1,0:T(8,128)(2,1)}, f32[128,128]{1,0:T(8,128)}, f32[128,128]{1,0:T(8,128)}) custom-call(bf16[128,1024]{1,0:T(8,128)(2,1)S(1)} %get-tuple-element.7.out_in, bf16[128,1024]{1,0:T(8,128)(2,1)S(1)} %get-tuple-element.8.dq_in, bf16[2,2,2,64,128]{4,3,2,1,0:T(8,128)(2,1)S(1)} %get-tuple-element.9.terms), custom_call_target="tpu_custom_call" | custom-call | tf_op jit(solution)/shard_map/pallas_call | solution.py:348

commit v3 on v2

--- a/solution.py
+++ b/solution.py
@@ -34,6 +34,8 @@
     out_stage,
     dq_stage,
     term_stage,
+    weights,
+    dprobs_own,
     load_sem,
     kv_send,
     kv_recv,
@@ -135,53 +137,102 @@
 
     for load in loads[1:]:
         load.wait()
-    for j in range(1, halo + 1):
-
-        @pl.when(me - j >= 0)
-        def _():
-            for copy in kv_copies(j, me):
-                copy.wait_recv()
-
-        @pl.when(me - j < 0)
-        def _():
-            window[j - 1] = jnp.zeros(window.shape[1:], window.dtype)
-
-    key_win = jnp.concatenate([window[j - 1, 0] for j in range(halo, 0, -1)] + [k_ref[...]], axis=0)
-    value_win = jnp.concatenate(
-        [window[j - 1, 1] for j in range(halo, 0, -1)] + [v_ref[...]], axis=0
-    )
 
     def dot(a, b, contract):
         return lax.dot_general(
             a, b, (((contract[0],), (contract[1],)), ((), ())), preferred_element_type=jnp.float32
         )
 
-    def head(h, totals):
-        key_acc, value_acc = totals
-        at = pl.ds(pl.multiple_of(h * head_dim, head_dim), head_dim)
-        q_head = q_ref[:, at]
-        g_head = g_ref[:, at]
-        scores = dot(key_win, q_head, (1, 1)) + bias
-        top = jnp.max(scores, axis=0, keepdims=True)
-        raised = jnp.exp2((scores - top) * (scaling * math.log2(math.e)))
-        weights = raised * (1.0 / jnp.sum(raised, axis=0, keepdims=True))
-        probs = weights.astype(jnp.bfloat16)
-        dprobs = dot(value_win, g_head, (1, 1))
-        row_dot = jnp.sum(weights * dprobs, axis=0, keepdims=True)
-        dscores = (weights * (dprobs - row_dot)).astype(jnp.bfloat16)
-        out_stage[:, at] = dot(probs, value_win, (0, 0)).astype(jnp.bfloat16)
-        dq_stage[:, at] = (scaling * dot(dscores, key_win, (0, 0))).astype(jnp.bfloat16)
-        return (key_acc + dot(dscores, q_head, (1, 0)), value_acc + dot(probs, g_head, (1, 0)))
-
-    def row_copies(group, half, finish):
+    def columns_of(h):
+        return pl.ds(pl.multiple_of(h * head_dim, head_dim), head_dim)
+
+    def queries_of(h):
+        return pl.ds(pl.multiple_of(h * rows, rows), rows)
+
+    unrolled = rows * keys <= 256 * 256
+
+    def each_head(first, last, body, state):
+        if not unrolled:
+            return lax.fori_loop(first, last, body, state)
+        for h in range(first, last):
+            state = body(h, state)
+        return state
+
+    below = halo * rows
+    own = pl.ds(below, rows)
+    earlier = pl.ds(0, below)
+
+    def own_head(h, state):
+        scores = dot(k_ref[...], q_ref[:, columns_of(h)], (1, 1))
+        weights[own, queries_of(h)] = scores + bias[below:]
+        dprobs_own[:, queries_of(h)] = dot(v_ref[...], g_ref[:, columns_of(h)], (1, 1))
+        return state
+
+    each_head(0, heads, own_head, 0)
+
+    for j in range(1, halo + 1):
+
+        @pl.when(me - j >= 0)
+        def _():
+            for copy in kv_copies(j, me):
+                copy.wait_recv()
+
+        @pl.when(me - j < 0)
+        def _():
+            window[j - 1] = jnp.zeros(window.shape[1:], window.dtype)
+
+    key_low = jnp.concatenate([window[j - 1, 0] for j in range(halo, 0, -1)], axis=0)
+    value_low = jnp.concatenate([window[j - 1, 1] for j in range(halo, 0, -1)], axis=0)
+    key_win = jnp.concatenate([key_low, k_ref[...]], axis=0)
+    value_win = jnp.concatenate([value_low, v_ref[...]], axis=0)
+
+    def forward(group):
+        def head(h, state):
+            at = queries_of(h)
+            low = dot(key_low, q_ref[:, columns_of(h)], (1, 1)) + bias[:below]
+            scores = jnp.concatenate([low, weights[own, at]], axis=0)
+            top = jnp.max(scores, axis=0, keepdims=True)
+            raised = jnp.exp2((scores - top) * (scaling * math.log2(math.e)))
+            weight = raised * (1.0 / jnp.sum(raised, axis=0, keepdims=True))
+            weights[:, at] = weight
+            out = dot(weight.astype(jnp.bfloat16), value_win, (0, 0))
+            out_stage[group, :, columns_of(h - group * GROUP_HEADS)] = out.astype(jnp.bfloat16)
+            return state
+
+        return head
+
+    def backward(group):
+        def head(h, totals):
+            key_acc, value_acc = totals
+            at = queries_of(h)
+            q_head = q_ref[:, columns_of(h)]
+            g_head = g_ref[:, columns_of(h)]
+            weight = weights[:, at]
+            dprobs = jnp.concatenate([dot(value_low, g_head, (1, 1)), dprobs_own[:, at]], axis=0)
+            row_dot = jnp.sum(weight * dprobs, axis=0, keepdims=True)
+            dscores = (weight * (dprobs - row_dot)).astype(jnp.bfloat16)
+            query_part = scaling * dot(dscores, key_win, (0, 0))
+            dq_stage[group, :, columns_of(h - group * GROUP_HEADS)] = query_part.astype(jnp.bfloat16)
+            return (
+                key_acc + dot(dscores, q_head, (1, 0)),
+                value_acc + dot(weight.astype(jnp.bfloat16), g_head, (1, 0)),
+            )
+
+        return head
+
+    staged = ((out_stage, out_ref), (dq_stage, dq_ref))
+
+    def row_copy(i, group, half):
         target, slot = place(2 * me + half)
-        at = pl.ds(group * GROUP_HEADS * head_dim, GROUP_HEADS * head_dim)
         here = pl.ds(half * half_rows, half_rows)
         there = pl.ds(pl.multiple_of(slot * half_rows, half_rows), half_rows)
-        for i, (stage, result) in enumerate(((out_stage, out_ref), (dq_stage, dq_ref))):
-            src, dst = stage.at[here, at], result.at[there, at]
-            send, recv = row_send.at[group, half, i], row_recv.at[group, slot, i]
-            yield src, dst, send, recv, target
+        return (
+            staged[i][0].at[group, here],
+            staged[i][1].at[group, there],
+            row_send.at[group, half, i],
+            row_recv.at[group, slot, i],
+            target,
+        )
 
     def term_copy(j, half):
         target, slot = place(2 * (me - j) + half)
@@ -207,17 +258,17 @@
         def _():
             remote(src, dst, send, recv, target).wait_send()
 
+    for group in range(groups):
+        first = group * GROUP_HEADS
+        each_head(first, first + GROUP_HEADS, forward(group), 0)
+        for half in range(2):
+            start(*row_copy(0, group, half))
     totals = (jnp.zeros((keys, head_dim), jnp.float32),) * 2
     for group in range(groups):
         first = group * GROUP_HEADS
-        if rows * keys <= 256 * 256:
-            for h in range(first, first + GROUP_HEADS):
-                totals = head(h, totals)
-        else:
-            totals = lax.fori_loop(first, first + GROUP_HEADS, head, totals)
+        totals = each_head(first, first + GROUP_HEADS, backward(group), totals)
         for half in range(2):
-            for copy in row_copies(group, half, False):
-                start(*copy)
+            start(*row_copy(1, group, half))
 
     for i, total in enumerate((totals[0] * scaling, totals[1])):
         total = total.astype(jnp.bfloat16)
@@ -232,13 +283,12 @@
             for half in range(2):
                 start(*term_copy(j, half))
 
-    for group in range(groups):
-        at = pl.ds(group * GROUP_HEADS * head_dim, GROUP_HEADS * head_dim)
-        for slot in range(2):
-            there = pl.ds(slot * half_rows, half_rows)
-            for i, (stage, result) in enumerate(((out_stage, out_ref), (dq_stage, dq_ref))):
+    for i, (stage, result) in enumerate(staged):
+        for group in range(groups):
+            for slot in range(2):
+                there = pl.ds(slot * half_rows, half_rows)
                 pltpu.make_async_copy(
-                    stage.at[there, at], result.at[there, at], row_recv.at[group, slot, i]
+                    stage.at[group, there], result.at[group, there], row_recv.at[group, slot, i]
                 ).wait()
     for slot in range(2):
         for j in range(halo + 1):
@@ -262,8 +312,8 @@
 
     for group in range(groups):
         for half in range(2):
-            for copy in row_copies(group, half, True):
-                finish_send(*copy)
+            for i in range(2):
+                finish_send(*row_copy(i, group, half))
     for j in range(halo + 1):
 
         @pl.when(me - j >= 0)
@@ -272,11 +322,15 @@
                 finish_send(*term_copy(j, half))
 
 
-def finish(out_in, dq_in, terms, out_ref, dq_ref, dk_ref, dv_ref, grads, sems):
-    rows = [
-        pltpu.make_async_copy(out_in, out_ref, sems.at[0]),
-        pltpu.make_async_copy(dq_in, dq_ref, sems.at[1]),
-    ]
+def finish(out_in, dq_in, terms, out_ref, dq_ref, dk_ref, dv_ref, grads, row_sems, sems):
+    groups, _, group_width = out_in.shape
+    rows = []
+    for group in range(groups):
+        at = pl.ds(group * group_width, group_width)
+        for i, (src, dst) in enumerate(((out_in, out_ref), (dq_in, dq_ref))):
+            rows.append(
+                pltpu.make_async_copy(src.at[group], dst.at[:, at], row_sems.at[i, group])
+            )
     for copy in rows:
         copy.start()
     half_rows = terms.shape[3]
@@ -286,7 +340,7 @@
             for j in range(1, terms.shape[1]):
                 total += terms[slot, j, i].astype(jnp.float32)
             grads[i, pl.ds(slot * half_rows, half_rows), :] = total
-        copy = pltpu.make_async_copy(grads.at[i], result, sems.at[2 + i])
+        copy = pltpu.make_async_copy(grads.at[i], result, sems.at[i])
         copy.start()
         rows.append(copy)
     for copy in rows:
@@ -306,14 +360,15 @@
     anywhere = pl.BlockSpec(memory_space=pl.ANY)
     dma = pltpu.SemaphoreType.DMA
     keys = (halo + 1) * rows
+    group_shape = jax.ShapeDtypeStruct((groups, rows, GROUP_HEADS * head_dim), jnp.bfloat16)
     row_shape = jax.ShapeDtypeStruct((rows, width), jnp.bfloat16)
     grad_shape = jax.ShapeDtypeStruct((rows, head_dim), jnp.float32)
     operands = (queries, key_states, value_states, out_grad, docs)
     out_rows, dq_rows, terms = pl.pallas_call(
         functools.partial(kernel, members, halo),
         out_shape=(
-            row_shape,
-            row_shape,
+            group_shape,
+            group_shape,
             jax.ShapeDtypeStruct((2, halo + 1, 2, half_rows, head_dim), jnp.bfloat16),
         ),
         in_specs=[hbm] * 5,
@@ -325,9 +380,11 @@
             pltpu.VMEM((rows, width), jnp.bfloat16),
             pltpu.VMEM(docs.shape, jnp.int32),
             pltpu.VMEM((halo, 2, rows, head_dim), jnp.bfloat16),
-            pltpu.VMEM((rows, width), jnp.bfloat16),
-            pltpu.VMEM((rows, width), jnp.bfloat16),
+            pltpu.VMEM(group_shape.shape, jnp.bfloat16),
+            pltpu.VMEM(group_shape.shape, jnp.bfloat16),
             pltpu.VMEM((halo + 1, 2, 2, half_rows, head_dim), jnp.bfloat16),
+            pltpu.VMEM((keys, width // head_dim * rows), jnp.float32),
+            pltpu.VMEM((rows, width // head_dim * rows), jnp.float32),
             dma((5,)),
             dma((halo, 2)),
             dma((halo, 2)),
@@ -350,7 +407,7 @@
         out_shape=(row_shape, row_shape, grad_shape, grad_shape),
         in_specs=[anywhere, anywhere, vmem],
         out_specs=(hbm,) * 4,
-        scratch_shapes=[pltpu.VMEM((2, rows, head_dim), jnp.float32), dma((4,))],
+        scratch_shapes=[pltpu.VMEM((2, rows, head_dim), jnp.float32), dma((2, groups)), dma((2,))],
         compiler_params=pltpu.CompilerParams(vmem_limit_bytes=16 * 1024 * 1024),
     )(out_rows, dq_rows, terms)
 

time: 27 us -> 27.1 us (level)
  no operation moved by 1% of the time
where the time goes in v3:
time: 27.1 us; the launch traced here: 26.9 us
  Pallas kernels  26.3 us (97%)
  between operations  0.64 us (2%)
    pallas_call x1, Pallas kernels, shards(): pl.pallas_call(functools.partial(kernel, members, halo), out_shape=(group...  25.4 us
    pallas_call x1, Pallas kernels, shards(): pl.pallas_call(finish, out_shape=(row_shape, row_shape, grad_shape, grad_...  0.91 us

profile of v3, /device:TPU:0, one launch (start us, length us, event | category | flops | bytes accessed | tf_op | source)
XLA Modules:
  0.0 26.9 jit_solution(13265787200123659915)
XLA Ops:
  0.6 25.4 %shard_map.84 = (bf16[4,128,256]{2,1,0:T(8,128)(2,1)S(1)}, bf16[4,128,256]{2,1,0:T(8,128)(2,1)S(1)}, bf16[2,2,2,64,128]{4,3,2,1,0:T(8,128)(2,1)S(1)}) custom-call(bf16[128,1024]{1,0:T(8,128)(2,1)} %q_hbm.1, bf16[128,128]{1,0:T(8,128)(2,1)} %k_hbm.1, bf16[128,128]{1,0:T(8,128)(2,1)} %v_hbm.1, bf16[128,1024]{1,0:T(8,128)(2,1)} %g_hbm.1, s32[8,128]{1,0:T(8,128)} %bitcast.1), custom_call_target="tpu_custom_call" | custom-call | flops 402653184 | bytes 1245184 | tf_op jit(solution)/shard_map/pallas_call | solution.py:367
  26.0 0.9 %shard_map.85 = (bf16[128,1024]{1,0:T(8,128)(2,1)}, bf16[128,1024]{1,0:T(8,128)(2,1)}, f32[128,128]{1,0:T(8,128)}, f32[128,128]{1,0:T(8,128)}) custom-call(bf16[4,128,256]{2,1,0:T(8,128)(2,1)S(1)} %get-tuple-element.7.out_in, bf16[4,128,256]{2,1,0:T(8,128)(2,1)S(1)} %get-tuple-element.8.dq_in, bf16[2,2,2,64,128]{4,3,2,1,0:T(8,128)(2,1)S(1)} %get-tuple-element.9.terms), custom_call_target="tpu_custom_call" | custom-call | tf_op jit(solution)/shard_map/pallas_call | solution.py:405

commit v4 on v3

--- a/solution.py
+++ b/solution.py
@@ -10,7 +10,7 @@
 
 NEG_FILL = -1e30
 LANES = 128
-GROUP_HEADS = 2
+GROUP_HEADS = 4
 MESH = pl.DeviceIdType.MESH
 
 
@@ -65,9 +65,6 @@
             )
         )
     ]
-    for load in loads:
-        load.start()
-
     def place(block):
         upper = block >= members
         return jnp.where(upper, 2 * members - 1 - block, block), upper.astype(jnp.int32)
@@ -99,6 +96,8 @@
         for half in range(2):
             target, _ = place(2 * (me - j) + half)
             expected += ((me - j >= 0) & (target != me)).astype(jnp.int32)
+    for load in loads:
+        load.start()
     pl.semaphore_wait(barrier, expected)
 
     def kv_copies(j, target):

time: 27.1 us -> 27.4 us (1.011)
  Pallas kernels: 26.3 us -> 26.6 us
    pallas_call x1, Pallas kernels: 25.4 us -> 25.7 us  [shards(): pl.pallas_call(functools.partial(kernel, members, halo), out_shape=(group...]
where the time goes in v4:
time: 27.4 us; the launch traced here: 27.2 us
  Pallas kernels  26.6 us (97%)
  between operations  0.64 us (2%)
    pallas_call x1, Pallas kernels, shards(): pl.pallas_call(functools.partial(kernel, members, halo), out_shape=(group...  25.7 us
    pallas_call x1, Pallas kernels, shards(): pl.pallas_call(finish, out_shape=(row_shape, row_shape, grad_shape, grad_...  0.88 us

profile of v4, /device:TPU:0, one launch (start us, length us, event | category | flops | bytes accessed | tf_op | source)
XLA Modules:
  0.0 27.2 jit_solution(11782099159907386713)
XLA Ops:
  0.6 25.7 %shard_map.84 = (bf16[2,128,512]{2,1,0:T(8,128)(2,1)S(1)}, bf16[2,128,512]{2,1,0:T(8,128)(2,1)S(1)}, bf16[2,2,2,64,128]{4,3,2,1,0:T(8,128)(2,1)S(1)}) custom-call(bf16[128,1024]{1,0:T(8,128)(2,1)} %q_hbm.1, bf16[128,128]{1,0:T(8,128)(2,1)} %k_hbm.1, bf16[128,128]{1,0:T(8,128)(2,1)} %v_hbm.1, bf16[128,1024]{1,0:T(8,128)(2,1)} %g_hbm.1, s32[8,128]{1,0:T(8,128)} %bitcast.1), custom_call_target="tpu_custom_call" | custom-call | flops 402653184 | bytes 1245184 | tf_op jit(solution)/shard_map/pallas_call | solution.py:366
  26.4 0.9 %shard_map.85 = (bf16[128,1024]{1,0:T(8,128)(2,1)}, bf16[128,1024]{1,0:T(8,128)(2,1)}, f32[128,128]{1,0:T(8,128)}, f32[128,128]{1,0:T(8,128)}) custom-call(bf16[2,128,512]{2,1,0:T(8,128)(2,1)S(1)} %get-tuple-element.7.out_in, bf16[2,128,512]{2,1,0:T(8,128)(2,1)S(1)} %get-tuple-element.8.dq_in, bf16[2,2,2,64,128]{4,3,2,1,0:T(8,128)(2,1)S(1)} %get-tuple-element.9.terms), custom_call_target="tpu_custom_call" | custom-call | tf_op jit(solution)/shard_map/pallas_call | solution.py:404

commit v5 on v2

v5 whole, which is shorter than its diff:
```python
import functools
import math

import jax
import jax.numpy as jnp
from jax import lax
from jax.experimental import pallas as pl
from jax.experimental.pallas import tpu as pltpu
from jax.sharding import PartitionSpec as P

NEG_FILL = -1e30
LANES = 128
GROUP_HEADS = 2
MESH = pl.DeviceIdType.MESH


def dot(a, b, contract):
    return lax.dot_general(
        a, b, (((contract[0],), (contract[1],)), ((), ())), preferred_element_type=jnp.float32
    )


def kernel(
    members,
    span,
    q_hbm,
    k_hbm,
    v_hbm,
    g_hbm,
    doc_hbm,
    out_ref,
    dq_ref,
    own_terms,
    term_in,
    rows_in,
    window,
    doc_ref,
    doc_columns,
    bias,
    term_stage,
    load_sem,
    kv_send,
    kv_recv,
    relay_send,
    relay_recv,
    row_send,
    row_recv,
    term_send,
    term_recv,
):
    me = lax.axis_index("ctx")
    rows, width = q_hbm.shape
    head_dim = k_hbm.shape[1]
    size = rows // 2
    scaling = 1.0 / math.sqrt(head_dim)
    group_width = GROUP_HEADS * head_dim
    groups = width // group_width
    lanes = GROUP_HEADS * size
    keys = (span + 1) * size
    last = 2 * members - 1
    blocks = (me, last - me)

    def place(block):
        upper = block >= members
        return jnp.where(upper, last - block, block), upper.astype(jnp.int32)

    def remote(src, dst, send, recv, target):
        return pltpu.make_async_remote_copy(
            src_ref=src,
            dst_ref=dst,
            send_sem=send,
            recv_sem=recv,
            device_id={"ctx": target},
            device_id_type=MESH,
        )

    def flag(condition):
        return jnp.where(condition, 1, 0)

    def start(src, dst, send, recv, target, wanted=1):
        @pl.when(wanted * flag(target != me) == 1)
        def _():
            remote(src, dst, send, recv, target).start()

        @pl.when(wanted * flag(target == me) == 1)
        def _():
            pltpu.make_async_copy(src, dst, recv).start()

    def finish_send(src, dst, send, recv, target, wanted=1):
        @pl.when(wanted * flag(target != me) == 1)
        def _():
            remote(src, dst, send, recv, target).wait_send()

    def arrive(src, dst, recv):
        pltpu.make_async_copy(src, dst, recv).wait()

    barrier = pltpu.get_barrier_semaphore()

    def greet(device):
        pl.semaphore_signal(barrier, inc=1, device_id={"ctx": device}, device_id_type=MESH)

    expected = jnp.int32(0)
    for half in range(2):
        holder = blocks[half] // 2
        pl.when(holder != me)(functools.partial(greet, holder))
        target, _ = place(2 * me + half)
        expected += (target != me).astype(jnp.int32)
    for j in range(1, span + 1):
        pl.when(me - j >= 0)(functools.partial(greet, me - j))
        above, _ = place(me + j)
        pl.when(above != me)(functools.partial(greet, above))
        expected += (me - j >= 0).astype(jnp.int32) + (above != me).astype(jnp.int32)
    load = pltpu.make_async_copy(doc_hbm, doc_ref, load_sem)
    load.start()
    pl.semaphore_wait(barrier, expected)

    def kv_copy(i, half):
        target, slot = place(2 * me + half)
        return (
            (k_hbm, v_hbm)[i].at[pl.ds(half * size, size)],
            window.at[slot, span, i],
            kv_send.at[half, i],
            kv_recv.at[slot, i],
            target,
        )

    def row_copy(i, group, half):
        target, slot = place(2 * me + half)
        here = pl.ds(half * size, size)
        return (
            (q_hbm, g_hbm)[i].at[here, pl.ds(group * group_width, group_width)],
            rows_in.at[i, slot, group],
            row_send.at[i, half, group],
            row_recv.at[i, slot, group],
            target,
        )

    def relay_copy(slot, j):
        target, target_slot = place(blocks[slot] + j)
        return (
            window.at[slot, span],
            window.at[target_slot, span - j],
            relay_send.at[slot, j - 1],
            relay_recv.at[target_slot, j - 1],
            target,
        )

    def term_copy(slot, j):
        target, target_slot = place(blocks[slot] - j)
        return (
            term_stage.at[slot, j - 1],
            term_in.at[target_slot, j - 1],
            term_send.at[slot, j - 1],
            term_recv.at[target_slot, j - 1],
            target,
        )

    for half in range(2):
        for i in range(2):
            start(*kv_copy(i, half))
    for group in range(groups):
        for half in range(2):
            for i in range(2):
                start(*row_copy(i, group, half))

    load.wait()
    per_chunk = rows // LANES
    for slot, block in enumerate(blocks):
        chunk, odd = block // 2, block % 2
        row = jnp.concatenate(
            [doc_ref[pl.ds(chunk * per_chunk + i, 1), :] for i in range(per_chunk)], axis=1
        )
        turned = jnp.concatenate([row[:, size:], row[:, :size]], axis=1)
        query_doc = jnp.concatenate(
            [jnp.where(odd == 1, turned, row)[:, :size]] * GROUP_HEADS, axis=1
        )
        for back in range(span // 2, -1, -1):
            there = chunk - back
            for i in range(per_chunk):
                line = doc_ref[pl.ds(jnp.maximum(there, 0) * per_chunk + i, 1), :]
                column = jnp.broadcast_to(line, (LANES, LANES)).T
                low = ((span // 2 - back) * per_chunk + i) * LANES
                doc_columns[slot, low : low + LANES, :] = jnp.where(there >= 0, column, -1)
        key_doc = doc_columns[slot, pl.ds(pl.multiple_of(odd * size, size), keys), :]
        key_doc = jnp.concatenate([key_doc] * (lanes // LANES), axis=1)
        key_pos = lax.broadcasted_iota(jnp.int32, (keys, lanes), 0) - span * size
        query_pos = jnp.concatenate(
            [lax.broadcasted_iota(jnp.int32, (1, size), 1)] * GROUP_HEADS, axis=1
        )
        allowed = (key_doc == query_doc) & (key_pos <= query_pos)
        bias[slot] = jnp.where(allowed, 0.0, NEG_FILL)

    for slot, block in enumerate(blocks):
        for i, ref in enumerate((k_hbm, v_hbm)):
            arrive(ref.at[pl.ds(0, size)], window.at[slot, span, i], kv_recv.at[slot, i])
        for j in range(1, span + 1):
            start(*relay_copy(slot, j), flag(block + j <= last))

    for slot, block in enumerate(blocks):
        for j in range(1, span + 1):

            @pl.when(block - j >= 0)
            def _():
                arrive(
                    window.at[slot, span], window.at[slot, span - j], relay_recv.at[slot, j - 1]
                )

            @pl.when(block - j < 0)
            def _():
                window[slot, span - j] = jnp.zeros(window.shape[2:], window.dtype)

    totals = [(jnp.zeros((keys, head_dim), jnp.float32),) * 2 for _ in range(2)]

    def split(array):
        parts = [array[h * size : (h + 1) * size] for h in range(GROUP_HEADS)]
        return jnp.concatenate(parts, axis=1).astype(jnp.bfloat16)

    def stack(array):
        parts = [array[:, h * head_dim : (h + 1) * head_dim] for h in range(GROUP_HEADS)]
        return jnp.concatenate(parts, axis=0)

    for group in range(groups):
        at = pl.ds(group * group_width, group_width)
        for slot in range(2):
            for i, ref in enumerate((q_hbm, g_hbm)):
                arrive(
                    ref.at[pl.ds(0, size), at], rows_in.at[i, slot, group], row_recv.at[i, slot, group]
                )
        for slot in range(2):
            here = pl.ds(slot * size, size)
            key_win = jnp.concatenate([window[slot, p, 0] for p in range(span + 1)], axis=0)
            value_win = jnp.concatenate([window[slot, p, 1] for p in range(span + 1)], axis=0)
            query = stack(rows_in[0, slot, group])
            grad = stack(rows_in[1, slot, group])
            scores = dot(key_win, query, (1, 1)) + bias[slot]
            top = jnp.max(scores, axis=0, keepdims=True)
            raised = jnp.exp2((scores - top) * (scaling * math.log2(math.e)))
            weights = raised * (1.0 / jnp.sum(raised, axis=0, keepdims=True))
            probs = weights.astype(jnp.bfloat16)
            dprobs = dot(value_win, grad, (1, 1))
            row_dot = jnp.sum(weights * dprobs, axis=0, keepdims=True)
            dscores = (weights * (dprobs - row_dot)).astype(jnp.bfloat16)
            out_ref[here, at] = split(dot(probs, value_win, (0, 0)))
            dq_ref[here, at] = split(scaling * dot(dscores, key_win, (0, 0)))
            totals[slot] = (
                totals[slot][0] + dot(dscores, query, (1, 0)),
                totals[slot][1] + dot(probs, grad, (1, 0)),
            )

    for slot in range(2):
        for i, total in enumerate((totals[slot][0] * scaling, totals[slot][1])):
            own_terms[slot, i] = total[span * size :]
            for j in range(1, span + 1):
                low = (span - j) * size
                term_stage[slot, j - 1, i] = total[low : low + size].astype(jnp.bfloat16)
    for slot, block in enumerate(blocks):
        for j in range(1, span + 1):
            start(*term_copy(slot, j), flag(block - j >= 0))

    for half in range(2):
        for i in range(2):
            finish_send(*kv_copy(i, half))
            for group in range(groups):
                finish_send(*row_copy(i, group, half))
    for slot, block in enumerate(blocks):
        for j in range(1, span + 1):
            finish_send(*relay_copy(slot, j), flag(block + j <= last))

    for slot, block in enumerate(blocks):
        for j in range(1, span + 1):

            @pl.when(block + j <= last)
            def _():
                arrive(
                    term_stage.at[slot, j - 1], term_in.at[slot, j - 1], term_recv.at[slot, j - 1]
                )

            @pl.when(block + j > last)
            def _():
                term_in[slot, j - 1] = jnp.zeros(term_in.shape[2:], term_in.dtype)

    for slot, block in enumerate(blocks):
        for j in range(1, span + 1):
            finish_send(*term_copy(slot, j), flag(block - j >= 0))


def finish(out_in, dq_in, own_terms, terms, out_ref, dq_ref, dk_ref, dv_ref, grads, sems):
    copies = [
        pltpu.make_async_copy(out_in, out_ref, sems.at[0]),
        pltpu.make_async_copy(dq_in, dq_ref, sems.at[1]),
    ]
    for copy in copies:
        copy.start()
    size = terms.shape[3]
    for i, result in enumerate((dk_ref, dv_ref)):
        for slot in range(2):
            total = own_terms[slot, i]
            for j in range(terms.shape[1]):
                total += terms[slot, j, i].astype(jnp.float32)
            grads[i, pl.ds(slot * size, size), :] = total
        copy = pltpu.make_async_copy(grads.at[i], result, sems.at[2 + i])
        copy.start()
        copies.append(copy)
    for copy in copies:
        copy.wait()


def shards(queries, key_states, value_states, out_grad, doc_ids):
    members = lax.axis_size("ctx")
    rows, width = queries.shape
    head_dim = key_states.shape[1]
    size = rows // 2
    span = members // 4
    groups = width // head_dim // GROUP_HEADS
    keys = (span + 1) * size
    docs = doc_ids.reshape(doc_ids.shape[0] // LANES, LANES)
    vmem = pl.BlockSpec(memory_space=pltpu.VMEM)
    hbm = pl.BlockSpec(memory_space=pltpu.HBM)
    anywhere = pl.BlockSpec(memory_space=pl.ANY)
    dma = pltpu.SemaphoreType.DMA
    row_shape = jax.ShapeDtypeStruct((rows, width), jnp.bfloat16)
    grad_shape = jax.ShapeDtypeStruct((rows, head_dim), jnp.float32)
    operands = (queries, key_states, value_states, out_grad, docs)
    results = pl.pallas_call(
        functools.partial(kernel, members, span),
        out_shape=(
            row_shape,
            row_shape,
            jax.ShapeDtypeStruct((2, 2, size, head_dim), jnp.float32),
            jax.ShapeDtypeStruct((2, span, 2, size, head_dim), jnp.bfloat16),
        ),
        in_specs=[hbm] * 5,
        out_specs=(vmem,) * 4,
        scratch_shapes=[
            pltpu.VMEM((2, 2, groups, size, GROUP_HEADS * head_dim), jnp.bfloat16),
            pltpu.VMEM((2, span + 1, 2, size, head_dim), jnp.bfloat16),
            pltpu.VMEM(docs.shape, jnp.int32),
            pltpu.VMEM((2, (span + 2) * size, LANES), jnp.int32),
            pltpu.VMEM((2, keys, GROUP_HEADS * size), jnp.float32),
            pltpu.VMEM((2, span, 2, size, head_dim), jnp.bfloat16),
            dma,
            dma((2, 2)),
            dma((2, 2)),
            dma((2, span)),
            dma((2, span)),
            dma((2, 2, groups)),
            dma((2, 2, groups)),
            dma((2, span)),
            dma((2, span)),
        ],
        compiler_params=pltpu.CompilerParams(
            collective_id=0, has_side_effects=True, vmem_limit_bytes=40 * 1024 * 1024
        ),
        cost_estimate=pl.CostEstimate(
            flops=12 * rows * keys * width,
            bytes_accessed=8 * rows * width + 12 * rows * head_dim,
            transcendentals=rows * keys * width // head_dim,
        ),
    )(*(pltpu.with_memory_space_constraint(x, pltpu.HBM) for x in operands))
    return pl.pallas_call(
        finish,
        out_shape=(row_shape, row_shape, grad_shape, grad_shape),
        in_specs=[anywhere, anywhere, vmem, vmem],
        out_specs=(hbm,) * 4,
        scratch_shapes=[pltpu.VMEM((2, rows, head_dim), jnp.float32), dma((4,))],
        compiler_params=pltpu.CompilerParams(vmem_limit_bytes=16 * 1024 * 1024),
    )(*results)


def solution(mesh):
    placed = P(("grp", "ctx"), None)
    return jax.shard_map(
        shards,
        mesh=mesh,
        in_specs=(placed, placed, placed, placed, P("grp")),
        out_specs=(placed,) * 4,
        check_vma=False,
    )
```

time: 27 us -> 29.7 us (1.100)
  Pallas kernels: 26.3 us -> 28.9 us
    pallas_call x1, Pallas kernels: 25.4 us -> 28 us  [shards(): pl.pallas_call(functools.partial(kernel, members, span), out_shape=(row_s...]
where the time goes in v5:
time: 29.7 us; the launch traced here: 29.5 us
  Pallas kernels  28.9 us (97%)
  between operations  0.64 us (2%)
    pallas_call x1, Pallas kernels, shards(): pl.pallas_call(functools.partial(kernel, members, span), out_shape=(row_s...  28 us
    pallas_call x1, Pallas kernels, shards(): pl.pallas_call(finish, out_shape=(row_shape, row_shape, grad_shape, grad_...  0.86 us

profile of v5, /device:TPU:0, one launch (start us, length us, event | category | flops | bytes accessed | tf_op | source)
XLA Modules:
  0.0 29.5 jit_solution(10894833096220716819)
XLA Ops:
  0.6 28.0 %shard_map.84 = (bf16[128,1024]{1,0:T(8,128)(2,1)S(1)}, bf16[128,1024]{1,0:T(8,128)(2,1)S(1)}, f32[2,2,64,128]{3,2,1,0:T(8,128)S(1)}, bf16[2,2,2,64,128]{4,3,2,1,0:T(8,128)(2,1)S(1)}) custom-call(bf16[128,1024]{1,0:T(8,128)(2,1)} %q_hbm.1, bf16[128,128]{1,0:T(8,128)(2,1)} %k_hbm.1, bf16[128,128]{1,0:T(8,128)(2,1)} %v_hbm.1, bf16[128,1024]{1,0:T(8,128)(2,1)} %g_hbm.1, ...), custom_call_target="tpu_custom_call" | custom-call | flops 301989888 | bytes 1245184 | tf_op jit(solution)/shard_map/pallas_call | solution.py:324
  28.7 0.9 %shard_map.85 = (bf16[128,1024]{1,0:T(8,128)(2,1)}, bf16[128,1024]{1,0:T(8,128)(2,1)}, f32[128,128]{1,0:T(8,128)}, f32[128,128]{1,0:T(8,128)}) custom-call(bf16[128,1024]{1,0:T(8,128)(2,1)S(1)} %get-tuple-element.8.out_in, bf16[128,1024]{1,0:T(8,128)(2,1)S(1)} %get-tuple-element.9.dq_in, f32[2,2,64,128]{3,2,1,0:T(8,128)S(1)} %get-tuple-element.10.own_terms, ...), custom_call_target="tpu_custom_call" | custom-call | tf_op jit(solution)/shard_map/pallas_call | solution.py:360

commit v6 on v5

--- a/solution.py
+++ b/solution.py
@@ -158,10 +158,13 @@
     for half in range(2):
         for i in range(2):
             start(*kv_copy(i, half))
-    for group in range(groups):
+
+    def send_rows(group):
         for half in range(2):
             for i in range(2):
                 start(*row_copy(i, group, half))
+
+    send_rows(0)
 
     load.wait()
     per_chunk = rows // LANES
@@ -195,6 +198,8 @@
             arrive(ref.at[pl.ds(0, size)], window.at[slot, span, i], kv_recv.at[slot, i])
         for j in range(1, span + 1):
             start(*relay_copy(slot, j), flag(block + j <= last))
+    for group in range(1, groups):
+        send_rows(group)
 
     for slot, block in enumerate(blocks):
         for j in range(1, span + 1):

time: 29.7 us -> 27.2 us (0.916)
  Pallas kernels: 28.9 us -> 26.4 us
    pallas_call x1, Pallas kernels: 28 us -> 25.5 us  [shards(): pl.pallas_call(functools.partial(kernel, members, span), out_shape=(row_s...]
where the time goes in v6:
time: 27.2 us; the launch traced here: 27 us
  Pallas kernels  26.4 us (97%)
  between operations  0.64 us (2%)
    pallas_call x1, Pallas kernels, shards(): pl.pallas_call(functools.partial(kernel, members, span), out_shape=(row_s...  25.5 us
    pallas_call x1, Pallas kernels, shards(): pl.pallas_call(finish, out_shape=(row_shape, row_shape, grad_shape, grad_...  0.86 us

profile of v6, /device:TPU:0, one launch (start us, length us, event | category | flops | bytes accessed | tf_op | source)
XLA Modules:
  0.0 27.0 jit_solution(15824671335532178276)
XLA Ops:
  0.6 25.5 %shard_map.84 = (bf16[128,1024]{1,0:T(8,128)(2,1)S(1)}, bf16[128,1024]{1,0:T(8,128)(2,1)S(1)}, f32[2,2,64,128]{3,2,1,0:T(8,128)S(1)}, bf16[2,2,2,64,128]{4,3,2,1,0:T(8,128)(2,1)S(1)}) custom-call(bf16[128,1024]{1,0:T(8,128)(2,1)} %q_hbm.1, bf16[128,128]{1,0:T(8,128)(2,1)} %k_hbm.1, bf16[128,128]{1,0:T(8,128)(2,1)} %v_hbm.1, bf16[128,1024]{1,0:T(8,128)(2,1)} %g_hbm.1, ...), custom_call_target="tpu_custom_call" | custom-call | flops 301989888 | bytes 1245184 | tf_op jit(solution)/shard_map/pallas_call | solution.py:329
  26.2 0.9 %shard_map.85 = (bf16[128,1024]{1,0:T(8,128)(2,1)}, bf16[128,1024]{1,0:T(8,128)(2,1)}, f32[128,128]{1,0:T(8,128)}, f32[128,128]{1,0:T(8,128)}) custom-call(bf16[128,1024]{1,0:T(8,128)(2,1)S(1)} %get-tuple-element.8.out_in, bf16[128,1024]{1,0:T(8,128)(2,1)S(1)} %get-tuple-element.9.dq_in, f32[2,2,64,128]{3,2,1,0:T(8,128)S(1)} %get-tuple-element.10.own_terms, ...), custom_call_target="tpu_custom_call" | custom-call | tf_op jit(solution)/shard_map/pallas_call | solution.py:365

commit v7 on v6

--- a/solution.py
+++ b/solution.py
@@ -224,17 +224,37 @@
         parts = [array[:, h * head_dim : (h + 1) * head_dim] for h in range(GROUP_HEADS)]
         return jnp.concatenate(parts, axis=0)
 
+    def send_terms(slot):
+        for i, total in enumerate((totals[slot][0] * scaling, totals[slot][1])):
+            own_terms[slot, i] = total[span * size :]
+            for j in range(1, span + 1):
+                low = (span - j) * size
+                term_stage[slot, j - 1, i] = total[low : low + size].astype(jnp.bfloat16)
+        for j in range(1, span + 1):
+            start(*term_copy(slot, j), flag(blocks[slot] - j >= 0))
+
+    def windows(slot):
+        return [
+            jnp.concatenate([window[slot, p, i] for p in range(span + 1)], axis=0)
+            for i in range(2)
+        ]
+
+    def write_rows(group, slot, probs, dscores):
+        here = pl.ds(slot * size, size)
+        at = pl.ds(group * group_width, group_width)
+        key_win, value_win = windows(slot)
+        out_ref[here, at] = split(dot(probs, value_win, (0, 0)))
+        dq_ref[here, at] = split(scaling * dot(dscores, key_win, (0, 0)))
+
     for group in range(groups):
         at = pl.ds(group * group_width, group_width)
+        later = []
         for slot in range(2):
             for i, ref in enumerate((q_hbm, g_hbm)):
                 arrive(
                     ref.at[pl.ds(0, size), at], rows_in.at[i, slot, group], row_recv.at[i, slot, group]
                 )
-        for slot in range(2):
-            here = pl.ds(slot * size, size)
-            key_win = jnp.concatenate([window[slot, p, 0] for p in range(span + 1)], axis=0)
-            value_win = jnp.concatenate([window[slot, p, 1] for p in range(span + 1)], axis=0)
+            key_win, value_win = windows(slot)
             query = stack(rows_in[0, slot, group])
             grad = stack(rows_in[1, slot, group])
             scores = dot(key_win, query, (1, 1)) + bias[slot]
@@ -245,22 +265,17 @@
             dprobs = dot(value_win, grad, (1, 1))
             row_dot = jnp.sum(weights * dprobs, axis=0, keepdims=True)
             dscores = (weights * (dprobs - row_dot)).astype(jnp.bfloat16)
-            out_ref[here, at] = split(dot(probs, value_win, (0, 0)))
-            dq_ref[here, at] = split(scaling * dot(dscores, key_win, (0, 0)))
             totals[slot] = (
                 totals[slot][0] + dot(dscores, query, (1, 0)),
                 totals[slot][1] + dot(probs, grad, (1, 0)),
             )
-
-    for slot in range(2):
-        for i, total in enumerate((totals[slot][0] * scaling, totals[slot][1])):
-            own_terms[slot, i] = total[span * size :]
-            for j in range(1, span + 1):
-                low = (span - j) * size
-                term_stage[slot, j - 1, i] = total[low : low + size].astype(jnp.bfloat16)
-    for slot, block in enumerate(blocks):
-        for j in range(1, span + 1):
-            start(*term_copy(slot, j), flag(block - j >= 0))
+            if group < groups - 1:
+                write_rows(group, slot, probs, dscores)
+            else:
+                send_terms(slot)
+                later.append((probs, dscores))
+        for slot, kept in enumerate(later):
+            write_rows(group, slot, *kept)
 
     for half in range(2):
         for i in range(2):

time: 27.2 us -> 25.9 us (0.952)
  Pallas kernels: 26.4 us -> 25.1 us
    pallas_call x1, Pallas kernels: 25.5 us -> 24.2 us  [shards(): pl.pallas_call(functools.partial(kernel, members, span), out_shape=(row_s...]
where the time goes in v7:
time: 25.9 us; the launch traced here: 25.7 us
  Pallas kernels  25.1 us (97%)
  between operations  0.64 us (2%)
    pallas_call x1, Pallas kernels, shards(): pl.pallas_call(functools.partial(kernel, members, span), out_shape=(row_s...  24.2 us
    pallas_call x1, Pallas kernels, shards(): pl.pallas_call(finish, out_shape=(row_shape, row_shape, grad_shape, grad_...  0.86 us

profile of v7, /device:TPU:0, one launch (start us, length us, event | category | flops | bytes accessed | tf_op | source)
XLA Modules:
  0.0 25.7 jit_solution(6251486755432284162)
XLA Ops:
  0.6 24.2 %shard_map.84 = (bf16[128,1024]{1,0:T(8,128)(2,1)S(1)}, bf16[128,1024]{1,0:T(8,128)(2,1)S(1)}, f32[2,2,64,128]{3,2,1,0:T(8,128)S(1)}, bf16[2,2,2,64,128]{4,3,2,1,0:T(8,128)(2,1)S(1)}) custom-call(bf16[128,1024]{1,0:T(8,128)(2,1)} %q_hbm.1, bf16[128,128]{1,0:T(8,128)(2,1)} %k_hbm.1, bf16[128,128]{1,0:T(8,128)(2,1)} %v_hbm.1, bf16[128,1024]{1,0:T(8,128)(2,1)} %g_hbm.1, ...), custom_call_target="tpu_custom_call" | custom-call | flops 301989888 | bytes 1245184 | tf_op jit(solution)/shard_map/pallas_call | solution.py:344
  24.9 0.9 %shard_map.85 = (bf16[128,1024]{1,0:T(8,128)(2,1)}, bf16[128,1024]{1,0:T(8,128)(2,1)}, f32[128,128]{1,0:T(8,128)}, f32[128,128]{1,0:T(8,128)}) custom-call(bf16[128,1024]{1,0:T(8,128)(2,1)S(1)} %get-tuple-element.8.out_in, bf16[128,1024]{1,0:T(8,128)(2,1)S(1)} %get-tuple-element.9.dq_in, f32[2,2,64,128]{3,2,1,0:T(8,128)S(1)} %get-tuple-element.10.own_terms, ...), custom_call_target="tpu_custom_call" | custom-call | tf_op jit(solution)/shard_map/pallas_call | solution.py:380

commit v8 on v7

--- a/solution.py
+++ b/solution.py
@@ -165,6 +165,7 @@
                 start(*row_copy(i, group, half))
 
     send_rows(0)
+    send_rows(1)
 
     load.wait()
     per_chunk = rows // LANES
@@ -198,7 +199,7 @@
             arrive(ref.at[pl.ds(0, size)], window.at[slot, span, i], kv_recv.at[slot, i])
         for j in range(1, span + 1):
             start(*relay_copy(slot, j), flag(block + j <= last))
-    for group in range(1, groups):
+    for group in range(2, groups):
         send_rows(group)
 
     for slot, block in enumerate(blocks):

time: 25.9 us -> 25.7 us (level)
  Pallas kernels: 25.1 us -> 24.8 us
where the time goes in v8:
time: 25.7 us; the launch traced here: 25.5 us
  Pallas kernels  24.8 us (96%)
  between operations  0.64 us (2%)
    pallas_call x1, Pallas kernels, shards(): pl.pallas_call(functools.partial(kernel, members, span), out_shape=(row_s...  24 us
    pallas_call x1, Pallas kernels, shards(): pl.pallas_call(finish, out_shape=(row_shape, row_shape, grad_shape, grad_...  0.86 us

profile of v8, /device:TPU:0, one launch (start us, length us, event | category | flops | bytes accessed | tf_op | source)
XLA Modules:
  0.0 25.5 jit_solution(7530956400007765039)
XLA Ops:
  0.6 24.0 %shard_map.84 = (bf16[128,1024]{1,0:T(8,128)(2,1)S(1)}, bf16[128,1024]{1,0:T(8,128)(2,1)S(1)}, f32[2,2,64,128]{3,2,1,0:T(8,128)S(1)}, bf16[2,2,2,64,128]{4,3,2,1,0:T(8,128)(2,1)S(1)}) custom-call(bf16[128,1024]{1,0:T(8,128)(2,1)} %q_hbm.1, bf16[128,128]{1,0:T(8,128)(2,1)} %k_hbm.1, bf16[128,128]{1,0:T(8,128)(2,1)} %v_hbm.1, bf16[128,1024]{1,0:T(8,128)(2,1)} %g_hbm.1, ...), custom_call_target="tpu_custom_call" | custom-call | flops 301989888 | bytes 1245184 | tf_op jit(solution)/shard_map/pallas_call | solution.py:345
  24.6 0.9 %shard_map.85 = (bf16[128,1024]{1,0:T(8,128)(2,1)}, bf16[128,1024]{1,0:T(8,128)(2,1)}, f32[128,128]{1,0:T(8,128)}, f32[128,128]{1,0:T(8,128)}) custom-call(bf16[128,1024]{1,0:T(8,128)(2,1)S(1)} %get-tuple-element.8.out_in, bf16[128,1024]{1,0:T(8,128)(2,1)S(1)} %get-tuple-element.9.dq_in, f32[2,2,64,128]{3,2,1,0:T(8,128)S(1)} %get-tuple-element.10.own_terms, ...), custom_call_target="tpu_custom_call" | custom-call | tf_op jit(solution)/shard_map/pallas_call | solution.py:381
